TPU v7x, 32 devices: a whole 2x2x4 slice. The times are simulated.
32 devices in a mesh: groups: 2 (over y), seq: 16 (over z, x, core).
Axes of the slice: x: 2, y: 2, z: 4, core: 2. Of those that a mesh axis runs over, the one named last changes fastest.
Arguments:
- queries: bfloat16 [4096, 24, 128], P(('groups', 'seq')), parts along dimension 0, may hold values from -72 to 72
- key_heads: bfloat16 [4096, 4, 128], P(('groups', 'seq')), parts along dimension 0, may hold values from -4 to 4
- value_heads: bfloat16 [4096, 4, 128], P(('groups', 'seq')), parts along dimension 0, may hold values from -6 to 6
- grad_out: bfloat16 [4096, 24, 128], P(('groups', 'seq')), parts along dimension 0, may hold values from -6 to 6
- offsets: int32 [2], replicated, may hold values from 1 to 8, as said below
- random_masks: int32 [1], replicated, may hold values from 1 to 15
- global_blocks: int32 [1], replicated, may hold values from 0 to 15
Outputs:
- attended: bfloat16 [4096, 24, 128], P(('groups', 'seq')), parts along dimension 0
- grad_queries: bfloat16 [4096, 24, 128], P(('groups', 'seq')), parts along dimension 0
- grad_keys: bfloat16 [4096, 4, 128], P(('groups', 'seq')), parts along dimension 0
- grad_values: bfloat16 [4096, 4, 128], P(('groups', 'seq')), parts along dimension 0
There are 2 independent parts, one for each index of `groups`. A program takes and returns all parts, laid end to end along the dimension named above; an argument that names none is the same for every part. Nothing has to cross between parts.
Inputs may be any that keep to these rules, and one draw needn't show every extreme that they name: `offsets`: distinct powers of two; one of them is 8.
All inputs are finite; a program needn't handle non-finite values.
Results may differ from a plain program's by a relative error of at most 0.012.
Values may be sent and summed in bfloat16 or wider, within the bound.
A program may use at most 64 MiB of HBM per device.

v0:
```python
import jax
import jax.numpy as jnp
from jax import lax
from jax.sharding import PartitionSpec as P


def from_partner(x, axis, distance):
    return lax.ppermute(x, axis, [(i, i ^ 1 << distance) for i in range(lax.axis_size(axis))])


def broadcast(value, axis, source):
    kept = jnp.where(lax.axis_index(axis) == source, value, 0).astype(value.dtype)
    return lax.psum(kept, axis)


def forward_head(inputs):
    query_part, key_part, value_part = inputs
    scale = query_part.shape[-1] ** (-0.5)
    scores = (
        jnp.einsum("qpd,kd->pqk", query_part, key_part, preferred_element_type=jnp.float32) * scale
    )
    top_score = jnp.max(scores, axis=-1, keepdims=True)
    log_total = top_score[..., 0] + jnp.log(jnp.sum(jnp.exp(scores - top_score), axis=-1))
    probs = jnp.exp(scores - log_total[..., None]).astype(jnp.bfloat16)
    output_part = jnp.einsum("pqk,kd->qpd", probs, value_part, preferred_element_type=jnp.float32)
    return (output_part.astype(jnp.bfloat16), log_total)


def backward_head(inputs):
    query_part, key_part, value_part, grad_part, output_part, log_total = inputs
    scale = query_part.shape[-1] ** (-0.5)
    scores = (
        jnp.einsum("qpd,kd->pqk", query_part, key_part, preferred_element_type=jnp.float32) * scale
    )
    weights = jnp.exp(scores - log_total[..., None])
    probs = weights.astype(jnp.bfloat16)
    deltas = jnp.sum(grad_part.astype(jnp.float32) * output_part.astype(jnp.float32), axis=-1).T
    value_terms = jnp.einsum("pqk,qpd->kd", probs, grad_part, preferred_element_type=jnp.float32)
    grad_probs = jnp.einsum(
        "qpd,kd->pqk", grad_part, value_part, preferred_element_type=jnp.float32
    )
    grad_scores = (weights * (grad_probs - deltas[..., None])).astype(jnp.bfloat16)
    grad_query = (
        jnp.einsum("pqk,kd->qpd", grad_scores, key_part, preferred_element_type=jnp.float32) * scale
    )
    key_terms = (
        jnp.einsum("pqk,qpd->kd", grad_scores, query_part, preferred_element_type=jnp.float32)
        * scale
    )
    return (grad_query.astype(jnp.bfloat16), key_terms, value_terms)


def kv_hop(tensor, bit_number):
    return from_partner(tensor, "seq", bit_number)


def grad_hop(tensor, bit_number):
    return from_partner(tensor.astype(jnp.bfloat16), "seq", bit_number).astype(tensor.dtype)


def bit_sequence():
    width_bits = lax.axis_size("seq").bit_length() - 1
    return list(range(width_bits))


def route(tensor, distance, hop):
    for bit_number in bit_sequence():
        tensor = lax.cond(
            jnp.bitwise_and(jnp.right_shift(distance, bit_number), 1) == 1,
            lambda moved, bit_number=bit_number: hop(moved, bit_number),
            lambda moved: moved,
            tensor,
        )
    return tensor


def fetch_blocks(stacked, distances, global_blocks):
    fetched = [stacked]
    for position in range(distances.shape[0]):
        fetched.append(route(stacked, distances[position], kv_hop))
    position = 0
    fetched.append(broadcast(stacked, "seq", global_blocks[position]))
    return jnp.stack(fetched)


def head_major(fetched, which):
    listed, rows, kv_count, width = (
        fetched.shape[0],
        fetched.shape[2],
        fetched.shape[3],
        fetched.shape[4],
    )
    return fetched[:, which].reshape(listed * rows, kv_count, width).transpose(1, 0, 2)


def local(queries, key_heads, value_heads, grad_out, offsets, random_masks, global_blocks):
    rows, heads, width = queries.shape
    kv_count = key_heads.shape[1]
    grouped = heads // kv_count
    distances = jnp.concatenate([offsets, random_masks])
    routed_count = distances.shape[0]
    stacked = jnp.stack([key_heads, value_heads])
    query_part = queries.reshape(rows, kv_count, grouped, width).transpose(1, 0, 2, 3)
    grad_part = grad_out.reshape(rows, kv_count, grouped, width).transpose(1, 0, 2, 3)
    fetched = fetch_blocks(stacked, distances, global_blocks)
    output_part, log_total = lax.map(
        forward_head, (query_part, head_major(fetched, 0), head_major(fetched, 1))
    )
    listed = fetched.shape[0]
    grad_query, key_terms, value_terms = lax.map(
        backward_head,
        (
            query_part,
            head_major(fetched, 0),
            head_major(fetched, 1),
            grad_part,
            output_part,
            log_total,
        ),
    )
    terms = (
        jnp.stack([key_terms, value_terms])
        .reshape(2, kv_count, listed, rows, width)
        .transpose(2, 0, 3, 1, 4)
    )
    totals = terms[0]
    for position in range(routed_count):
        totals = totals + route(terms[1 + position], distances[position], grad_hop)
    summed = lax.psum(terms[1 + routed_count :], "seq")
    owner = lax.axis_index("seq")
    position = 0
    totals = totals + jnp.where(
        owner == global_blocks[position], summed[position], jnp.float32(0.0)
    )
    attended = output_part.transpose(1, 0, 2, 3).reshape(rows, heads, width)
    grad_queries = grad_query.transpose(1, 0, 2, 3).reshape(rows, heads, width)
    grad_keys = totals[0].astype(jnp.bfloat16)
    grad_values = totals[1].astype(jnp.bfloat16)
    return (attended, grad_queries, grad_keys, grad_values)


def solution(mesh):
    return jax.shard_map(
        local,
        mesh=mesh,
        in_specs=(
            P(("groups", "seq"), None, None),
            P(("groups", "seq"), None, None),
            P(("groups", "seq"), None, None),
            P(("groups", "seq"), None, None),
            P(),
            P(),
            P(),
        ),
        out_specs=(
            P(("groups", "seq"), None, None),
            P(("groups", "seq"), None, None),
            P(("groups", "seq"), None, None),
            P(("groups", "seq"), None, None),
        ),
        check_vma=False,
    )
```

profile of v0, /device:TPU:0, one launch (start us, length us, event | category | flops | bytes accessed | tf_op | source)
XLA Modules:
  0.0 329.6 jit_solution(17306852728246045865)
XLA Ops:
  18.9 10.6 %conditional.26 = (bf16[2,128,4,128]{3,2,1,0:T(4,128)(2,1)}) conditional(s32[]{:T(128)} %bitcast.37, bf16[2,128,4,128]{3,2,1,0:T(4,128)(2,1)} %get-tuple-element.491, bf16[2,128,4,128]{3,2,1,0:T(4,128)(2,1)} %get-tuple-element.491), branch_computations={%region_4.0_spmd, %region_5.0_spmd} | conditional | bytes 1572912 | solution.py:68
  21.9 6.9 %collective-permute-done.2 = bf16[2,128,4,128]{3,2,1,0:T(4,128)(2,1)S(1)} collective-permute-done((bf16[2,128,4,128]{3,2,1,0:T(4,128)(2,1)}, bf16[2,128,4,128]{3,2,1,0:T(4,128)(2,1)S(1)}, u32[]{:S(2)}, u32[]{:S(2)}) %collective-permute-start.2) | collective-permute-done | bytes 262176 | tf_op jit(solution)/shard_map/cond/branch_1_fun/ppermute | solution.py:8
  29.5 15.7 %conditional.31 = (bf16[1,2,128,4,128]{4,3,2,1,0:T(4,128)(2,1)}) conditional(s32[]{:T(128)} %bitcast.40, bf16[2,128,4,128]{3,2,1,0:T(4,128)(2,1)} %get-tuple-element.495, bf16[2,128,4,128]{3,2,1,0:T(4,128)(2,1)} %get-tuple-element.495), branch_computations={%region_14.0_spmd, %region_15.0_spmd} | conditional | bytes 1572912 | solution.py:68
  32.4 12.1 %collective-permute-done.7 = bf16[2,128,4,128]{3,2,1,0:T(4,128)(2,1)S(1)} collective-permute-done((bf16[2,128,4,128]{3,2,1,0:T(4,128)(2,1)}, bf16[2,128,4,128]{3,2,1,0:T(4,128)(2,1)S(1)}, u32[]{:S(2)}, u32[]{:S(2)}) %collective-permute-start.7) | collective-permute-done | bytes 262176 | tf_op jit(solution)/shard_map/cond/branch_1_fun/ppermute | solution.py:8
  48.8 8.5 %conditional.33 = (bf16[2,128,4,128]{3,2,1,0:T(4,128)(2,1)}) conditional(s32[]{:T(128)} %bitcast.46, bf16[2,128,4,128]{3,2,1,0:T(4,128)(2,1)} %get-tuple-element.496, bf16[2,128,4,128]{3,2,1,0:T(4,128)(2,1)} %get-tuple-element.496), branch_computations={%region_18.0_spmd, %region_19.0_spmd} | conditional | bytes 1572912 | solution.py:68
  50.3 6.3 %collective-permute-done.9 = bf16[2,128,4,128]{3,2,1,0:T(4,128)(2,1)S(1)} collective-permute-done((bf16[2,128,4,128]{3,2,1,0:T(4,128)(2,1)}, bf16[2,128,4,128]{3,2,1,0:T(4,128)(2,1)S(1)}, u32[]{:S(2)}, u32[]{:S(2)}) %collective-permute-start.9) | collective-permute-done | bytes 262176 | tf_op jit(solution)/shard_map/cond/branch_1_fun/ppermute | solution.py:8
  57.3 8.3 %conditional.34 = (bf16[2,128,4,128]{3,2,1,0:T(4,128)(2,1)}) conditional(s32[]{:T(128)} %bitcast.45, bf16[2,128,4,128]{3,2,1,0:T(4,128)(2,1)} %get-tuple-element.497, bf16[2,128,4,128]{3,2,1,0:T(4,128)(2,1)} %get-tuple-element.497), branch_computations={%region_20.0_spmd, %region_21.0_spmd} | conditional | bytes 1572912 | solution.py:68
  58.8 6.1 %collective-permute-done.10 = bf16[2,128,4,128]{3,2,1,0:T(4,128)(2,1)S(1)} collective-permute-done((bf16[2,128,4,128]{3,2,1,0:T(4,128)(2,1)}, bf16[2,128,4,128]{3,2,1,0:T(4,128)(2,1)S(1)}, u32[]{:S(2)}, u32[]{:S(2)}) %collective-permute-start.10) | collective-permute-done | bytes 262176 | tf_op jit(solution)/shard_map/cond/branch_1_fun/ppermute | solution.py:8
  67.0 15.5 %conditional.35 = (bf16[1,2,128,4,128]{4,3,2,1,0:T(4,128)(2,1)}) conditional(s32[]{:T(128)} %bitcast.44, bf16[2,128,4,128]{3,2,1,0:T(4,128)(2,1)} %get-tuple-element.498, bf16[2,128,4,128]{3,2,1,0:T(4,128)(2,1)} %get-tuple-element.498), branch_computations={%region_22.0_spmd, %region_23.0_spmd} | conditional | bytes 1572912 | solution.py:68
  70.3 11.5 %collective-permute-done.11 = bf16[2,128,4,128]{3,2,1,0:T(4,128)(2,1)S(1)} collective-permute-done((bf16[2,128,4,128]{3,2,1,0:T(4,128)(2,1)}, bf16[2,128,4,128]{3,2,1,0:T(4,128)(2,1)S(1)}, u32[]{:S(2)}, u32[]{:S(2)}) %collective-permute-start.11) | collective-permute-done | bytes 262176 | tf_op jit(solution)/shard_map/cond/branch_1_fun/ppermute | solution.py:8
  83.6 27.9 %all-reduce.3.cloned.1.call-done = bf16[1,2,128,4,128]{4,3,2,1,0:T(4,128)(2,1)} async-done(((bf16[1,2,128,4,128]{4,3,2,1,0:T(4,128)(2,1)}), bf16[1,2,128,4,128]{4,3,2,1,0:T(4,128)(2,1)}) %all-reduce.3.cloned.1.call-update) | async-done | bytes 262160 | tf_op jit(solution)/shard_map/psum | solution.py:13
  114.4 7.9 %while.26 = (s32[]{:T(128)}, bf16[4,128,6,128]{1,3,2,0:T(8,128)(2,1)}, f32[4,6,128]{2,1,0:T(8,128)S(1)}, bf16[4,640,128]{2,1,0:T(8,128)(2,1)S(1)}, bf16[4,640,12...) while((s32[]{:T(128)}, bf16[4,128,6,128]{1,3,2,0:T(8,128)(2,1)}, ...), condition=%wide.region_28.29_spmd, body=%wide.region_25.28_spmd.sunk | while | flops 255687936 | bytes 6650969 | solution.py:106
  123.4 92.9 %while.27 = (s32[]{:T(128)}, bf16[4,128,6,128]{1,3,2,0:T(8,128)(2,1)}, f32[4,640,128]{2,0,1:T(4,128)}, f32[4,640,128]{2,0,1:T(4,128)}, bf16[4,640,128]{2,1,0:T(8...) while((s32[]{:T(128)}, ...), condition=%wide.region_31.32_spmd, body=%wide.region_29.31_spmd.sunk | while | flops 633748736 | bytes 13492377 | solution.py:110
  127.6 9.5 %dynamic_update_slice.29 = f32[4,640,128]{2,0,1:T(4,128)} dynamic-update-slice(f32[4,640,128]{2,0,1:T(4,128)} %get-tuple-element.468, f32[1,640,128]{2,0,1:T(1,128)S(1)} %bitcast.228, s32[]{:T(128)S(6)} %copy.100, s32[]{:T(128)} %constant.90.clone.1..sunk, s32[]{:T(128)} %constant.90.clone.1..sunk) | dynamic-update-slice | bytes 655364 | tf_op jit(solution)/shard_map/while/body/jit(dynamic_update_index_in_dim)/dynamic_update_slice | solution.py:110
  137.1 9.5 %dynamic_update_slice.30 = f32[4,640,128]{2,0,1:T(4,128)} dynamic-update-slice(f32[4,640,128]{2,0,1:T(4,128)} %get-tuple-element.469, f32[1,640,128]{2,0,1:T(1,128)S(1)} %bitcast.229, s32[]{:T(128)S(6)} %copy.100, s32[]{:T(128)} %constant.90.clone.1..sunk, s32[]{:T(128)} %constant.90.clone.1..sunk) | dynamic-update-slice | bytes 655364 | tf_op jit(solution)/shard_map/while/body/jit(dynamic_update_index_in_dim)/dynamic_update_slice | solution.py:110
  150.9 9.5 %dynamic_update_slice.29 = f32[4,640,128]{2,0,1:T(4,128)} dynamic-update-slice(f32[4,640,128]{2,0,1:T(4,128)} %get-tuple-element.468, f32[1,640,128]{2,0,1:T(1,128)S(1)} %bitcast.228, s32[]{:T(128)S(6)} %copy.100, s32[]{:T(128)} %constant.90.clone.1..sunk, s32[]{:T(128)} %constant.90.clone.1..sunk) | dynamic-update-slice | bytes 655364 | tf_op jit(solution)/shard_map/while/body/jit(dynamic_update_index_in_dim)/dynamic_update_slice | solution.py:110
  160.4 9.5 %dynamic_update_slice.30 = f32[4,640,128]{2,0,1:T(4,128)} dynamic-update-slice(f32[4,640,128]{2,0,1:T(4,128)} %get-tuple-element.469, f32[1,640,128]{2,0,1:T(1,128)S(1)} %bitcast.229, s32[]{:T(128)S(6)} %copy.100, s32[]{:T(128)} %constant.90.clone.1..sunk, s32[]{:T(128)} %constant.90.clone.1..sunk) | dynamic-update-slice | bytes 655364 | tf_op jit(solution)/shard_map/while/body/jit(dynamic_update_index_in_dim)/dynamic_update_slice | solution.py:110
  174.1 9.5 %dynamic_update_slice.29 = f32[4,640,128]{2,0,1:T(4,128)} dynamic-update-slice(f32[4,640,128]{2,0,1:T(4,128)} %get-tuple-element.468, f32[1,640,128]{2,0,1:T(1,128)S(1)} %bitcast.228, s32[]{:T(128)S(6)} %copy.100, s32[]{:T(128)} %constant.90.clone.1..sunk, s32[]{:T(128)} %constant.90.clone.1..sunk) | dynamic-update-slice | bytes 655364 | tf_op jit(solution)/shard_map/while/body/jit(dynamic_update_index_in_dim)/dynamic_update_slice | solution.py:110
  183.6 9.5 %dynamic_update_slice.30 = f32[4,640,128]{2,0,1:T(4,128)} dynamic-update-slice(f32[4,640,128]{2,0,1:T(4,128)} %get-tuple-element.469, f32[1,640,128]{2,0,1:T(1,128)S(1)} %bitcast.229, s32[]{:T(128)S(6)} %copy.100, s32[]{:T(128)} %constant.90.clone.1..sunk, s32[]{:T(128)} %constant.90.clone.1..sunk) | dynamic-update-slice | bytes 655364 | tf_op jit(solution)/shard_map/while/body/jit(dynamic_update_index_in_dim)/dynamic_update_slice | solution.py:110
  197.3 9.5 %dynamic_update_slice.29 = f32[4,640,128]{2,0,1:T(4,128)} dynamic-update-slice(f32[4,640,128]{2,0,1:T(4,128)} %get-tuple-element.468, f32[1,640,128]{2,0,1:T(1,128)S(1)} %bitcast.228, s32[]{:T(128)S(6)} %copy.100, s32[]{:T(128)} %constant.90.clone.1..sunk, s32[]{:T(128)} %constant.90.clone.1..sunk) | dynamic-update-slice | bytes 655364 | tf_op jit(solution)/shard_map/while/body/jit(dynamic_update_index_in_dim)/dynamic_update_slice | solution.py:110
  206.8 9.5 %dynamic_update_slice.30 = f32[4,640,128]{2,0,1:T(4,128)} dynamic-update-slice(f32[4,640,128]{2,0,1:T(4,128)} %get-tuple-element.469, f32[1,640,128]{2,0,1:T(1,128)S(1)} %bitcast.229, s32[]{:T(128)S(6)} %copy.100, s32[]{:T(128)} %constant.90.clone.1..sunk, s32[]{:T(128)} %constant.90.clone.1..sunk) | dynamic-update-slice | bytes 655364 | tf_op jit(solution)/shard_map/while/body/jit(dynamic_update_index_in_dim)/dynamic_update_slice | solution.py:110
  224.1 10.0 %conditional.45 = (f32[2,128,4,128]{3,2,1,0:T(4,128)S(1)}) conditional(s32[]{:T(128)} %bitcast.46, f32[2,128,4,128]{3,2,1,0:T(4,128)S(1)} %get-tuple-element.507, f32[2,128,4,128]{3,2,1,0:T(4,128)S(1)} %get-tuple-element.507), branch_computations={%region_50.51_spmd, %region_51.52_spmd} | conditional | flops 262144 | bytes 2621488 | solution.py:68
  224.9 9.2 %collective-permute-done.21 = bf16[2,128,4,128]{3,2,1,0:T(4,128)(2,1)S(1)} collective-permute-done((bf16[2,128,4,128]{3,2,1,0:T(4,128)(2,1)S(1)}, bf16[2,128,4,128]{3,2,1,0:T(4,128)(2,1)S(1)}, u32[]{:S(2)}, u32[]{:S(2)}) %collective-permute-start.21) | collective-permute-done | bytes 262176 | tf_op jit(solution)/shard_map/cond/branch_1_fun/ppermute | solution.py:8
  234.1 9.5 %conditional.46 = (f32[2,128,4,128]{3,2,1,0:T(4,128)S(1)}) conditional(s32[]{:T(128)} %bitcast.45, f32[2,128,4,128]{3,2,1,0:T(4,128)S(1)} %get-tuple-element.508, f32[2,128,4,128]{3,2,1,0:T(4,128)S(1)} %get-tuple-element.508), branch_computations={%region_52.53_spmd, %region_53.54_spmd} | conditional | flops 262144 | bytes 2621488 | solution.py:68
  234.4 9.3 %collective-permute-done.22 = bf16[2,128,4,128]{3,2,1,0:T(4,128)(2,1)S(1)} collective-permute-done((bf16[2,128,4,128]{3,2,1,0:T(4,128)(2,1)S(1)}, bf16[2,128,4,128]{3,2,1,0:T(4,128)(2,1)S(1)}, u32[]{:S(2)}, u32[]{:S(2)}) %collective-permute-start.22) | collective-permute-done | bytes 262176 | tf_op jit(solution)/shard_map/cond/branch_1_fun/ppermute | solution.py:8
  243.6 14.2 %conditional.47 = (f32[2,128,4,128]{3,2,1,0:T(4,128)S(1)}) conditional(s32[]{:T(128)} %bitcast.44, f32[2,128,4,128]{3,2,1,0:T(4,128)S(1)} %get-tuple-element.509, f32[2,128,4,128]{3,2,1,0:T(4,128)S(1)} %get-tuple-element.509), branch_computations={%region_54.55_spmd, %region_55.56_spmd} | conditional | flops 262144 | bytes 2621488 | solution.py:68
  243.8 13.9 %collective-permute-done.23 = bf16[2,128,4,128]{3,2,1,0:T(4,128)(2,1)S(1)} collective-permute-done((bf16[2,128,4,128]{3,2,1,0:T(4,128)(2,1)S(1)}, bf16[2,128,4,128]{3,2,1,0:T(4,128)(2,1)S(1)}, u32[]{:S(2)}, u32[]{:S(2)}) %collective-permute-start.23) | collective-permute-done | bytes 262176 | tf_op jit(solution)/shard_map/cond/branch_1_fun/ppermute | solution.py:8
  257.9 13.0 %conditional.43 = (f32[2,128,4,128]{3,2,1,0:T(4,128)S(1)}) conditional(s32[]{:T(128)} %bitcast.40, f32[2,128,4,128]{3,2,1,0:T(4,128)S(1)} %get-tuple-element.505, f32[2,128,4,128]{3,2,1,0:T(4,128)S(1)} %get-tuple-element.505), branch_computations={%region_46.47_spmd, %region_47.48_spmd} | conditional | flops 262144 | bytes 2621488 | solution.py:68
  258.1 12.8 %collective-permute-done.19 = bf16[2,128,4,128]{3,2,1,0:T(4,128)(2,1)S(1)} collective-permute-done((bf16[2,128,4,128]{3,2,1,0:T(4,128)(2,1)S(1)}, bf16[2,128,4,128]{3,2,1,0:T(4,128)(2,1)S(1)}, u32[]{:S(2)}, u32[]{:S(2)}) %collective-permute-start.19) | collective-permute-done | bytes 262176 | tf_op jit(solution)/shard_map/cond/branch_1_fun/ppermute | solution.py:8
  270.9 8.5 %conditional.38 = (f32[2,128,4,128]{3,2,1,0:T(4,128)S(1)}) conditional(s32[]{:T(128)} %bitcast.37, f32[2,128,4,128]{3,2,1,0:T(4,128)S(1)} %get-tuple-element.500, f32[2,128,4,128]{3,2,1,0:T(4,128)S(1)} %get-tuple-element.500), branch_computations={%region_36.37_spmd, %region_37.38_spmd} | conditional | flops 262144 | bytes 2621488 | solution.py:68
  271.1 8.2 %collective-permute-done.14 = bf16[2,128,4,128]{3,2,1,0:T(4,128)(2,1)S(1)} collective-permute-done((bf16[2,128,4,128]{3,2,1,0:T(4,128)(2,1)S(1)}, bf16[2,128,4,128]{3,2,1,0:T(4,128)(2,1)S(1)}, u32[]{:S(2)}, u32[]{:S(2)}) %collective-permute-start.14) | collective-permute-done | bytes 262176 | tf_op jit(solution)/shard_map/cond/branch_1_fun/ppermute | solution.py:8
  279.4 41.2 %all-reduce.5.cloned.1.call-done = f32[1,2,128,4,128]{4,3,2,1,0:T(4,128)} async-done(((f32[1,2,128,4,128]{4,3,2,1,0:T(4,128)}), f32[1,2,128,4,128]{4,3,2,1,0:T(4,128)}) %all-reduce.5.cloned.1.call-update) | async-done | bytes 524304 | tf_op jit(solution)/shard_map/psum | solution.py:129
  (127 shorter events, 69.4 us)
Async XLA Ops:
  7.2 104.3 %all-reduce.3.cloned.1.call-start = ((), (), s32[]{:S(2)}) async-start(), calls=%async_computation | async-start | bytes 524288 | tf_op jit(solution)/shard_map/psum | solution.py:13
  9.8 310.7 %all-reduce.5.cloned.1.call-start = ((), (), s32[]{:S(2)}) async-start(), calls=%async_computation.1 | async-start | bytes 1048576 | tf_op jit(solution)/shard_map/psum | solution.py:129
  18.9 9.9 %collective-permute-start.2 = (bf16[2,128,4,128]{3,2,1,0:T(4,128)(2,1)}, bf16[2,128,4,128]{3,2,1,0:T(4,128)(2,1)S(1)}, u32[]{:S(2)}, u32[]{:S(2)}) collective-permute-start(bf16[2,128,4,128]{3,2,1,0:T(4,128)(2,1)} %param.5), channel_id=1, source_target_pairs={{0,4},{1,5},{2,6},{3,7},{4,0},{5,1},{6,2},{7,3},{8,12},{9,13},{10,... | collective-permute-start | bytes 786440 | tf_op jit(solution)/shard_map/cond/branch_1_fun/ppermute | solution.py:8
  29.5 36.0 %copy-start.2 = (bf16[128,24,128]{2,1,0:T(8,128)(2,1)S(1)}, bf16[128,24,128]{2,1,0:T(8,128)(2,1)}, u32[]{:S(2)}) copy-start(bf16[128,24,128]{2,1,0:T(8,128)(2,1)} %param.59) | copy-start | bytes 2359300
  29.5 15.0 %collective-permute-start.7 = (bf16[2,128,4,128]{3,2,1,0:T(4,128)(2,1)}, bf16[2,128,4,128]{3,2,1,0:T(4,128)(2,1)S(1)}, u32[]{:S(2)}, u32[]{:S(2)}) collective-permute-start(bf16[2,128,4,128]{3,2,1,0:T(4,128)(2,1)} %param.15), channel_id=1, source_target_pairs={{0,8},{1,9},{2,10},{3,11},{4,12},{5,13},{6,14},{7,15},{8,0},{9,1},... | collective-permute-start | bytes 786440 | tf_op jit(solution)/shard_map/cond/branch_1_fun/ppermute | solution.py:8
  48.8 7.8 %collective-permute-start.9 = (bf16[2,128,4,128]{3,2,1,0:T(4,128)(2,1)}, bf16[2,128,4,128]{3,2,1,0:T(4,128)(2,1)S(1)}, u32[]{:S(2)}, u32[]{:S(2)}) collective-permute-start(bf16[2,128,4,128]{3,2,1,0:T(4,128)(2,1)} %param.19), channel_id=1, source_target_pairs={{0,2},{1,3},{2,0},{3,1},{4,6},{5,7},{6,4},{7,5},{8,10},{9,11},{10,... | collective-permute-start | bytes 786440 | tf_op jit(solution)/shard_map/cond/branch_1_fun/ppermute | solution.py:8
  57.3 7.6 %collective-permute-start.10 = (bf16[2,128,4,128]{3,2,1,0:T(4,128)(2,1)}, bf16[2,128,4,128]{3,2,1,0:T(4,128)(2,1)S(1)}, u32[]{:S(2)}, u32[]{:S(2)}) collective-permute-start(bf16[2,128,4,128]{3,2,1,0:T(4,128)(2,1)} %param.21), channel_id=1, source_target_pairs={{0,4},{1,5},{2,6},{3,7},{4,0},{5,1},{6,2},{7,3},{8,12},{9,13},{10,... | collective-permute-start | bytes 786440 | tf_op jit(solution)/shard_map/cond/branch_1_fun/ppermute | solution.py:8
  67.1 14.8 %collective-permute-start.11 = (bf16[2,128,4,128]{3,2,1,0:T(4,128)(2,1)}, bf16[2,128,4,128]{3,2,1,0:T(4,128)(2,1)S(1)}, u32[]{:S(2)}, u32[]{:S(2)}) collective-permute-start(bf16[2,128,4,128]{3,2,1,0:T(4,128)(2,1)} %param.23), channel_id=1, source_target_pairs={{0,8},{1,9},{2,10},{3,11},{4,12},{5,13},{6,14},{7,15},{8,0},{9,1},... | collective-permute-start | bytes 786440 | tf_op jit(solution)/shard_map/cond/branch_1_fun/ppermute | solution.py:8
  218.7 1.7 copy-start
  220.4 2.5 copy-start.1
  224.2 9.9 %collective-permute-start.21 = (bf16[2,128,4,128]{3,2,1,0:T(4,128)(2,1)S(1)}, bf16[2,128,4,128]{3,2,1,0:T(4,128)(2,1)S(1)}, u32[]{:S(2)}, u32[]{:S(2)}) collective-permute-start(bf16[2,128,4,128]{3,2,1,0:T(4,128)(2,1)S(1)} %convert_element_type.164), channel_id=1, source_target_pairs={{0,2},{1,3},{2,0},{3,1},{4,6},{5,7},{6,4},{7,5},{8,10},{9,11},{10,... | collective-permute-start | bytes 786440 | tf_op jit(solution)/shard_map/cond/branch_1_fun/ppermute | solution.py:8
  234.2 9.4 %collective-permute-start.22 = (bf16[2,128,4,128]{3,2,1,0:T(4,128)(2,1)S(1)}, bf16[2,128,4,128]{3,2,1,0:T(4,128)(2,1)S(1)}, u32[]{:S(2)}, u32[]{:S(2)}) collective-permute-start(bf16[2,128,4,128]{3,2,1,0:T(4,128)(2,1)S(1)} %convert_element_type.166), channel_id=1, source_target_pairs={{0,4},{1,5},{2,6},{3,7},{4,0},{5,1},{6,2},{7,3},{8,12},{9,13},{10,... | collective-permute-start | bytes 786440 | tf_op jit(solution)/shard_map/cond/branch_1_fun/ppermute | solution.py:8
  243.8 14.0 %collective-permute-start.23 = (bf16[2,128,4,128]{3,2,1,0:T(4,128)(2,1)S(1)}, bf16[2,128,4,128]{3,2,1,0:T(4,128)(2,1)S(1)}, u32[]{:S(2)}, u32[]{:S(2)}) collective-permute-start(bf16[2,128,4,128]{3,2,1,0:T(4,128)(2,1)S(1)} %convert_element_type.168), channel_id=1, source_target_pairs={{0,8},{1,9},{2,10},{3,11},{4,12},{5,13},{6,14},{7,15},{8,0},{9,1},... | collective-permute-start | bytes 786440 | tf_op jit(solution)/shard_map/cond/branch_1_fun/ppermute | solution.py:8
  258.0 12.9 %collective-permute-start.19 = (bf16[2,128,4,128]{3,2,1,0:T(4,128)(2,1)S(1)}, bf16[2,128,4,128]{3,2,1,0:T(4,128)(2,1)S(1)}, u32[]{:S(2)}, u32[]{:S(2)}) collective-permute-start(bf16[2,128,4,128]{3,2,1,0:T(4,128)(2,1)S(1)} %convert_element_type.160), channel_id=1, source_target_pairs={{0,8},{1,9},{2,10},{3,11},{4,12},{5,13},{6,14},{7,15},{8,0},{9,1},... | collective-permute-start | bytes 786440 | tf_op jit(solution)/shard_map/cond/branch_1_fun/ppermute | solution.py:8
  271.0 8.3 %collective-permute-start.14 = (bf16[2,128,4,128]{3,2,1,0:T(4,128)(2,1)S(1)}, bf16[2,128,4,128]{3,2,1,0:T(4,128)(2,1)S(1)}, u32[]{:S(2)}, u32[]{:S(2)}) collective-permute-start(bf16[2,128,4,128]{3,2,1,0:T(4,128)(2,1)S(1)} %convert_element_type.150), channel_id=1, source_target_pairs={{0,4},{1,5},{2,6},{3,7},{4,0},{5,1},{6,2},{7,3},{8,12},{9,13},{10,... | collective-permute-start | bytes 786440 | tf_op jit(solution)/shard_map/cond/branch_1_fun/ppermute | solution.py:8
Sparse Core Ops, SparseCore 0:
  12.0 99.4 all-reduce.2
  220.5 99.9 all-reduce.4
where the time goes:
time: 328 us; the launch traced here: 330 us
  waiting for transfers between devices  165 us (50%)
  local copies, waits for them, and re-layouts  102 us (31%)
  between operations  20.7 us (6%)
  matrix products  18.1 us (6%)
  starting transfers between devices  13.3 us (4%)
  other arithmetic  9.57 us (3%)
    ppermute x10, waiting for transfers between devices, from_partner(): lax.ppermute(x, axis, [(i, i ^ 1 << distance) for i in range(lax.axis_siz...  96.2 us
    dynamic_update_slice x8, local copies, waits for them, and re-layouts, local(): lax.map(backward_head, (query_part, head_major(fetched, 0), head_major(fe...  75.9 us
    psum x1, waiting for transfers between devices, local(): summed = lax.psum(terms[1 + routed_count:], 'seq')  41.2 us
    psum x1, waiting for transfers between devices, broadcast(): return lax.psum(kept, axis)  27.9 us
    ppermute x10, starting transfers between devices, from_partner(): lax.ppermute(x, axis, [(i, i ^ 1 << distance) for i in range(lax.axis_siz...  13.2 us
    unnamed x13, local copies, waits for them, and re-layouts  8.94 us
  transfers between devices with their start and end apart: 12, of which 12 were waited for; matrix products, arithmetic and copies ran while one was open for 5% of the time, Pallas kernels for 0%

commit v1 on v0

--- a/solution.py
+++ b/solution.py
@@ -1,6 +1,8 @@
 import jax
 import jax.numpy as jnp
 from jax import lax
+from jax.experimental import pallas as pl
+from jax.experimental.pallas import tpu as pltpu
 from jax.sharding import PartitionSpec as P
 
 
@@ -93,7 +95,7 @@
     return fetched[:, which].reshape(listed * rows, kv_count, width).transpose(1, 0, 2)
 
 
-def local(queries, key_heads, value_heads, grad_out, offsets, random_masks, global_blocks):
+def local_any(queries, key_heads, value_heads, grad_out, offsets, random_masks, global_blocks):
     rows, heads, width = queries.shape
     kv_count = key_heads.shape[1]
     grouped = heads // kv_count
@@ -139,9 +141,396 @@
     return (attended, grad_queries, grad_keys, grad_values)
 
 
+MESH = pl.DeviceIdType.MESH
+FLOAT = jnp.float32
+HALF = jnp.bfloat16
+FAR, SIDE, CORES = 4, 2, 2
+
+
+def place():
+    me = lax.axis_index("seq")
+    return me, me // 4, (me // 2) % 2, me % 2
+
+
+def neighbours(me, z, x, c):
+    sibling = me + 1 - 2 * c
+    across = me + 2 - 4 * x
+    return sibling, across, me + 4, me - 4
+
+
+def greet(me, z, x, c):
+    sibling, across, up, down = neighbours(me, z, x, c)
+    barrier = pltpu.get_barrier_semaphore()
+    for other in (sibling, across):
+        pl.semaphore_signal(barrier, inc=1, device_id={"seq": other}, device_id_type=MESH)
+
+    @pl.when(z < FAR - 1)
+    def _():
+        pl.semaphore_signal(barrier, inc=1, device_id={"seq": up}, device_id_type=MESH)
+
+    @pl.when(z > 0)
+    def _():
+        pl.semaphore_signal(barrier, inc=1, device_id={"seq": down}, device_id_type=MESH)
+
+    pl.semaphore_wait(barrier, 3 + (z + 1) // 2 % 2)
+
+
+def gather_kernel(kv_ref, all_ref, own_sem, side_sem, core_sem, up_sem, down_sem, recv_sem):
+    me, z, x, c = place()
+    sibling, across, up, down = neighbours(me, z, x, c)
+
+    def copy(slot, half, sem, target, own=False):
+        return pltpu.make_async_remote_copy(
+            src_ref=kv_ref.at[half] if own else all_ref.at[slot, half],
+            dst_ref=all_ref.at[slot, half],
+            send_sem=sem,
+            recv_sem=recv_sem.at[slot, half],
+            device_id={"seq": target},
+            device_id_type=MESH,
+        )
+
+    def arrived(slot, half):
+        copy(slot, half, side_sem.at[0, half], across).wait_recv()
+
+    def column(row):
+        return row * 4 + x * 2 + c
+
+    def opposite(row):
+        return row * 4 + (1 - x) * 2 + c
+
+    greet(me, z, x, c)
+
+    def pass_on(row, half, upward, downward, own=False):
+        slot = column(row)
+        copy(slot, half, side_sem.at[row, half], across, own).start()
+        if upward:
+
+            @pl.when(z < FAR - 1)
+            def _():
+                copy(slot, half, up_sem.at[row, half], up, own).start()
+
+        if downward:
+
+            @pl.when(z > 0)
+            def _():
+                copy(slot, half, down_sem.at[row, half], down, own).start()
+
+        copy(slot, half, core_sem.at[0, row, half], sibling, own).start()
+
+    for half in range(2):
+        pass_on(z, half, True, True, own=True)
+        pltpu.make_async_copy(kv_ref.at[half], all_ref.at[me, half], own_sem.at[half]).start()
+
+    def share(row, half):
+        arrived(opposite(row), half)
+        copy(opposite(row), half, core_sem.at[1, row, half], sibling).start()
+
+    for step in range(1, FAR):
+        for half in range(2):
+
+            @pl.when(z - step >= 0)
+            def _(step=step, half=half):
+                arrived(column(z - step), half)
+                pass_on(z - step, half, True, False)
+
+            @pl.when(z + step < FAR)
+            def _(step=step, half=half):
+                arrived(column(z + step), half)
+                pass_on(z + step, half, False, True)
+
+            if step == 1:
+                share(z, half)
+            else:
+
+                @pl.when(z - step + 1 >= 0)
+                def _(step=step, half=half):
+                    share(z - step + 1, half)
+
+                @pl.when(z + step - 1 < FAR)
+                def _(step=step, half=half):
+                    share(z + step - 1, half)
+
+    for half in range(2):
+
+        @pl.when(z - FAR + 1 >= 0)
+        def _(half=half):
+            share(z - FAR + 1, half)
+
+        @pl.when(z + FAR - 1 < FAR)
+        def _(half=half):
+            share(z + FAR - 1, half)
+
+    for half in range(2):
+        for row in range(FAR):
+            for col in range(SIDE):
+                arrived(row * 4 + col * 2 + 1 - c, half)
+    for half in range(2):
+        pltpu.make_async_copy(kv_ref.at[half], all_ref.at[me, half], own_sem.at[half]).wait()
+        for row in range(FAR):
+            copy(column(row), half, side_sem.at[row, half], across).wait_send()
+            for which in range(2):
+                copy(column(row), half, core_sem.at[which, row, half], sibling).wait_send()
+
+            @pl.when((z < FAR - 1) & (z >= row))
+            def _(row=row, half=half):
+                copy(column(row), half, up_sem.at[row, half], up).wait_send()
+
+            @pl.when((z > 0) & (z <= row))
+            def _(row=row, half=half):
+                copy(column(row), half, down_sem.at[row, half], down).wait_send()
+
+
+def gather(kv):
+    dma = pltpu.SemaphoreType.DMA
+    return pl.pallas_call(
+        gather_kernel,
+        out_shape=jax.ShapeDtypeStruct((16, *kv.shape), kv.dtype),
+        in_specs=[pl.BlockSpec(memory_space=pl.ANY)],
+        out_specs=pl.BlockSpec(memory_space=pl.ANY),
+        scratch_shapes=[
+            dma((2,)),
+            dma((FAR, 2)),
+            dma((2, FAR, 2)),
+            dma((FAR, 2)),
+            dma((FAR, 2)),
+            dma((16, 2)),
+        ],
+        compiler_params=pltpu.CompilerParams(collective_id=0, has_side_effects=True),
+    )(kv)
+
+
+def nt(a, b):
+    return lax.dot_general(a, b, (((1,), (1,)), ((), ())), preferred_element_type=FLOAT)
+
+
+def nn(a, b):
+    return lax.dot_general(a, b, (((1,), (0,)), ((), ())), preferred_element_type=FLOAT)
+
+
+def attend_kernel(
+    chosen_ref, q_ref, g_ref, all_ref,
+    att_ref, dq_ref, own_ref, terms_ref,
+    qf, gf, af, df, sums,
+):
+    listed = chosen_ref.shape[0]
+    kv_count, rows, width = all_ref.shape[2], all_ref.shape[3], all_ref.shape[4]
+    heads = q_ref.shape[0] // rows
+    grouped = heads // kv_count
+    scale = width ** (-0.5)
+    qf[...] = q_ref[...].astype(FLOAT)
+    gf[...] = g_ref[...].astype(FLOAT)
+    terms_ref[...] = jnp.zeros_like(terms_ref)
+
+    def group(kv, _):
+        keys = jnp.concatenate([all_ref[chosen_ref[i], 0, kv] for i in range(listed)], axis=0)
+        values = jnp.concatenate([all_ref[chosen_ref[i], 1, kv] for i in range(listed)], axis=0)
+        keys_t, values_t = keys.T, values.T
+        for pair in range(grouped // 2):
+            first = kv * grouped + 2 * pair
+            spans = [pl.ds(first + i, rows, stride=heads) for i in range(2)]
+            query = jnp.concatenate([qf[s, :] for s in spans], axis=0).astype(HALF)
+            grad = jnp.concatenate([gf[s, :] for s in spans], axis=0).astype(HALF)
+            scores = nt(keys, query)
+            top = jnp.max(scores, axis=0, keepdims=True)
+            weights = jnp.exp((scores - top) * scale)
+            weights = weights * (1.0 / jnp.sum(weights, axis=0, keepdims=True))
+            probs = weights.astype(HALF)
+            out = nn(values_t, probs).T
+            grad_probs = nt(values, grad)
+            deltas = jnp.sum(weights * grad_probs, axis=0, keepdims=True)
+            grad_scores = (weights * (grad_probs - deltas)).astype(HALF)
+            grad_query = (nn(keys_t, grad_scores) * scale).T
+            for i, s in enumerate(spans):
+                af[s, :] = out[i * rows : (i + 1) * rows]
+                df[s, :] = grad_query[i * rows : (i + 1) * rows]
+            key_terms = nn(grad_scores, query)
+            value_terms = nn(probs, grad)
+            if pair == 0:
+                sums[0] = key_terms
+                sums[1] = value_terms
+            else:
+                sums[0] += key_terms
+                sums[1] += value_terms
+        for which, factor in ((0, scale), (1, 1.0)):
+            own_ref[which, kv] = sums[which, :rows] * factor
+            for i in range(1, listed):
+                term = sums[which, i * rows : (i + 1) * rows] * factor
+                block = chosen_ref[i]
+                terms_ref[block, which, kv] = (
+                    terms_ref[block, which, kv].astype(FLOAT) + term
+                ).astype(HALF)
+        return 0
+
+    lax.fori_loop(0, kv_count, group, 0)
+    att_ref[...] = af[...].astype(HALF)
+    dq_ref[...] = df[...].astype(HALF)
+
+
+def attend(chosen, query_rows, grad_rows, fetched):
+    total, width = query_rows.shape
+    _, _, kv_count, rows, _ = fetched.shape
+    listed = chosen.shape[0]
+    whole = pl.BlockSpec(memory_space=pltpu.VMEM)
+    return pl.pallas_call(
+        attend_kernel,
+        out_shape=(
+            jax.ShapeDtypeStruct((total, width), HALF),
+            jax.ShapeDtypeStruct((total, width), HALF),
+            jax.ShapeDtypeStruct((2, kv_count, rows, width), FLOAT),
+            jax.ShapeDtypeStruct(fetched.shape, HALF),
+        ),
+        in_specs=[pl.BlockSpec(memory_space=pltpu.SMEM), whole, whole, whole],
+        out_specs=(whole,) * 4,
+        scratch_shapes=[pltpu.VMEM((total, width), FLOAT)] * 4
+        + [pltpu.VMEM((2, listed * rows, width), FLOAT)],
+        compiler_params=pltpu.CompilerParams(vmem_limit_bytes=48 * 2**20),
+    )(chosen, query_rows, grad_rows, fetched)
+
+
+def pick(codes, z):
+    packed = sum(code * 4**i for i, code in enumerate(codes))
+    return packed // ((1 + 3 * (z % 2)) * (1 + 15 * (z // 2))) % 4
+
+
+ORDER = ((3, 3, 0, 0), (2, 0, 3, 1), (1, 2, 1, 2), (0, 1, 2, 3))
+
+
+def scatter_kernel(
+    terms_ref, own_ref, out_ref,
+    from_core, from_side, from_up, from_down, to_side, to_row, acc,
+    core_send, side_send, row_send, core_recv, side_recv, up_recv, down_recv,
+):
+    me, z, x, c = place()
+    sibling, across, up, down = neighbours(me, z, x, c)
+
+    def copy(src, dst, send, recv, target):
+        return pltpu.make_async_remote_copy(
+            src_ref=src, dst_ref=dst, send_sem=send, recv_sem=recv,
+            device_id={"seq": target}, device_id_type=MESH,
+        )
+
+    def core_copy(row, col, half):
+        return copy(
+            terms_ref.at[row * 4 + col * 2 + 1 - c, half], from_core.at[row, col, half],
+            core_send.at[row, col, half], core_recv.at[row, col, half], sibling,
+        )
+
+    def side_copy(row, half):
+        return copy(
+            to_side.at[row, half], from_side.at[row, half],
+            side_send.at[row, half], side_recv.at[row, half], across,
+        )
+
+    def up_copy(row, half):
+        return copy(
+            to_row.at[row, half], from_down.at[row, half],
+            row_send.at[row, half], down_recv.at[row, half], up,
+        )
+
+    def down_copy(row, half):
+        return copy(
+            to_row.at[row, half], from_up.at[row, half],
+            row_send.at[row, half], up_recv.at[row, half], down,
+        )
+
+    greet(me, z, x, c)
+    rows = [pick(codes, z) for codes in ORDER]
+    for row in rows:
+        for half in range(2):
+            core_copy(row, 1 - x, half).start()
+    for row in rows:
+        for half in range(2):
+            core_copy(row, x, half).start()
+    for row in rows:
+        for half in range(2):
+            core_copy(row, 1 - x, half).wait_recv()
+            to_side[row, half] = (
+                terms_ref[row * 4 + (1 - x) * 2 + c, half].astype(FLOAT)
+                + from_core[row, 1 - x, half].astype(FLOAT)
+            ).astype(HALF)
+            side_copy(row, half).start()
+    for step, row in enumerate(rows):
+        for half in range(2):
+            core_copy(row, x, half).wait_recv()
+            side_copy(row, half).wait_recv()
+            acc[...] = (
+                terms_ref[row * 4 + x * 2 + c, half].astype(FLOAT)
+                + from_core[row, x, half].astype(FLOAT)
+                + from_side[row, half].astype(FLOAT)
+            )
+
+            @pl.when((row >= z) & (z > 0))
+            def _(row=row, half=half):
+                up_copy(row, half).wait_recv()
+                acc[...] += from_down[row, half].astype(FLOAT)
+
+            @pl.when((row <= z) & (z < FAR - 1))
+            def _(row=row, half=half):
+                down_copy(row, half).wait_recv()
+                acc[...] += from_up[row, half].astype(FLOAT)
+
+            if step < FAR - 1:
+                to_row[row, half] = acc[...].astype(HALF)
+
+                @pl.when(row > z)
+                def _(row=row, half=half):
+                    up_copy(row, half).start()
+
+                @pl.when(row < z)
+                def _(row=row, half=half):
+                    down_copy(row, half).start()
+            else:
+                out_ref[half] = (acc[...] + own_ref[half]).astype(HALF)
+    for step, row in enumerate(rows):
+        for half in range(2):
+            side_copy(row, half).wait_send()
+            for col in range(SIDE):
+                core_copy(row, col, half).wait_send()
+            if step < FAR - 1:
+                up_copy(row, half).wait_send()
+
+
+def scatter(terms, own):
+    tile = own.shape[1:]
+    dma = pltpu.SemaphoreType.DMA
+    whole = pl.BlockSpec(memory_space=pltpu.VMEM)
+    slots = pltpu.VMEM((FAR, 2, *tile), HALF)
+    return pl.pallas_call(
+        scatter_kernel,
+        out_shape=jax.ShapeDtypeStruct(own.shape, HALF),
+        in_specs=[whole, whole],
+        out_specs=whole,
+        scratch_shapes=[
+            pltpu.VMEM((FAR, SIDE, 2, *tile), HALF),
+            slots, slots, slots, slots, slots,
+            pltpu.VMEM(tile, FLOAT),
+            dma((FAR, SIDE, 2)), dma((FAR, 2)), dma((FAR, 2)),
+            dma((FAR, SIDE, 2)), dma((FAR, 2)), dma((FAR, 2)), dma((FAR, 2)),
+        ],
+        compiler_params=pltpu.CompilerParams(
+            collective_id=1, has_side_effects=True, vmem_limit_bytes=40 * 2**20
+        ),
+    )(terms, own)
+
+
+def local(queries, key_heads, value_heads, grad_out, offsets, random_masks, global_blocks):
+    rows, heads, width = queries.shape
+    me = lax.axis_index("seq").astype(jnp.int32)
+    chosen = jnp.concatenate([me[None], me ^ offsets, me ^ random_masks, global_blocks])
+    kv = jnp.stack([key_heads, value_heads]).transpose(0, 2, 1, 3)
+    fetched = gather(kv)
+    attended, grad_queries, own, terms = attend(
+        chosen, queries.reshape(rows * heads, width), grad_out.reshape(rows * heads, width), fetched
+    )
+    totals = scatter(terms, own).transpose(0, 2, 1, 3)
+    return (
+        attended.reshape(queries.shape), grad_queries.reshape(queries.shape), totals[0], totals[1]
+    )
+
+
 def solution(mesh):
     return jax.shard_map(
-        local,
+        local if mesh.shape["seq"] == FAR * SIDE * CORES else local_any,
         mesh=mesh,
         in_specs=(
             P(("groups", "seq"), None, None),

time: 328 us -> 87.3 us (0.27)
  waiting for transfers between devices: 165 us -> 0 us
  local copies, waits for them, and re-layouts: 102 us -> 4.74 us
  Pallas kernels: 0 us -> 78.7 us
  between operations: 20.7 us -> 2.11 us
  matrix products: 18.1 us -> 0 us
  starting transfers between devices: 13.3 us -> 0 us
  other arithmetic: 9.57 us -> 1.47 us
    ppermute x10 -> x0, waiting for transfers between devices: 96.2 us -> none  [from_partner(): lax.ppermute(x, axis, [(i, i ^ 1 << distance) for i in range(lax.axis_siz...]
    pallas_call x0 -> x3, Pallas kernels: none -> 78.7 us  [the longest x1 30.1 us: gather(): pl.pallas_call(gather_kernel, out_shape=jax.ShapeDtypeStruct((16, *kv.sha...]
    dynamic_update_slice x8 -> x0, local copies, waits for them, and re-layouts: 75.9 us -> none  [local(): lax.map(backward_head, (query_part, head_major(fetched, 0), head_major(fe...]
    psum x2 -> x0, waiting for transfers between devices: 69.1 us -> none  [the longest x1 41.2 us: local(): summed = lax.psum(terms[1 + routed_count:], 'seq')]
    dot_general x28 -> x0, matrix products: 18.1 us -> none  [the longest x4 4.75 us: forward_head(): jnp.einsum('pqk,kd->qpd', probs, value_part, preferred_element_type=jnp.f...]
    ppermute x10 -> x0, starting transfers between devices: 13.2 us -> none  [from_partner(): lax.ppermute(x, axis, [(i, i ^ 1 << distance) for i in range(lax.axis_siz...]
    cond x8 -> x0, local copies, waits for them, and re-layouts: 5.57 us -> none
    unnamed x13 -> x8, local copies, waits for them, and re-layouts: 8.94 us -> 3.71 us
  transfers between devices with their start and end apart: 12 -> 0, of which waited for: 12 -> 0; matrix products, arithmetic and copies ran while one was open for 5% -> 0% of each run, Pallas kernels for 0% -> 0%
where the time goes in v1:
time: 87.3 us; the launch traced here: 87 us
  Pallas kernels  78.7 us (90%)
  local copies, waits for them, and re-layouts  4.74 us (5%)
  between operations  2.11 us (2%)
  other arithmetic  1.47 us (2%)
    pallas_call x1, Pallas kernels, gather(): pl.pallas_call(gather_kernel, out_shape=jax.ShapeDtypeStruct((16, *kv.sha...  30.1 us
    pallas_call x1, Pallas kernels, scatter(): pl.pallas_call(scatter_kernel, out_shape=jax.ShapeDtypeStruct(own.shape,...  27.5 us
    pallas_call x1, Pallas kernels, attend(): pl.pallas_call(attend_kernel, out_shape=(jax.ShapeDtypeStruct((total, wid...  21.1 us
    unnamed x8, local copies, waits for them, and re-layouts  3.71 us

profile of v1, /device:TPU:0, one launch (start us, length us, event | category | flops | bytes accessed | tf_op | source)
XLA Modules:
  0.0 87.0 jit_solution(1238309689585273606)
XLA Ops:
  0.6 0.0 copy-start.2
  0.6 0.0 copy-start.1
  2.1 0.7 broadcast_xor_fusion
  2.7 0.1 pad_add_fusion.chosen_ref
  2.8 1.0 %copy_bitcast_fusion = (bf16[1,128,4,128]{3,1,2,0:T(8,128)(2,1)S(1)}, bf16[1,128,4,128]{3,1,2,0:T(8,128)(2,1)S(1)}) fusion(bf16[128,4,128]{2,1,0:T(4,128)(2,1)} %param.9, bf16[128,4,128]{2,1,0:T(4,128)(2,1)} %param.8), kind=kLoop, calls=%fused_computation.3 | loop fusion | bytes 524288 | tf_op jit(solution)/shard_map/stack | solution.py:520
  3.8 0.7 maximum_bitcast_fusion.kv_ref
  4.5 30.1 %shard_map.102.all_ref = bf16[16,2,4,128,128]{4,3,2,1,0:T(8,128)(2,1)} custom-call(bf16[2,4,128,128]{3,2,1,0:T(8,128)(2,1)} %maximum_bitcast_fusion.kv_ref), custom_call_target="tpu_custom_call" | custom-call | tf_op jit(solution)/shard_map/pallas_call | solution.py:285
  34.6 0.0 copy-done.2
  34.6 0.0 copy-done.1
  34.6 21.1 %shard_map.103 = (bf16[3072,128]{1,0:T(8,128)(2,1)}, bf16[3072,128]{1,0:T(8,128)(2,1)}, f32[2,4,128,128]{3,2,1,0:T(8,128)S(1)}, bf16[16,2,4,128,128]{4,3,2,1,0:T(8,128)(2,1)}) custom-call(s32[5]{0:T(128)S(1)} %pad_add_fusion.chosen_ref, bf16[3072,128]{1,0:T(8,128)(2,1)S(1)} %bitcast.17, bf16[3072,128]{1,0:T(8,128)(2,1)S(1)} %bitcast.18, ...), custom_call_target="tpu_custom_call" | custom-call | tf_op jit(solution)/shard_map/pallas_call | solution.py:374
  55.8 0.0 copy-start
  55.8 2.2 %copy-done = bf16[16,2,4,128,128]{4,3,2,1,0:T(8,128)(2,1)S(1)} copy-done((bf16[16,2,4,128,128]{4,3,2,1,0:T(8,128)(2,1)S(1)}, bf16[16,2,4,128,128]{4,3,2,1,0:T(8,128)(2,1)}, u32[]{:S(2)}) %copy-start) | copy-done | bytes 4194328
  58.0 27.5 %shard_map.104 = bf16[2,4,128,128]{3,2,1,0:T(8,128)(2,1)S(1)} custom-call(bf16[16,2,4,128,128]{4,3,2,1,0:T(8,128)(2,1)S(1)} %copy-done, f32[2,4,128,128]{3,2,1,0:T(8,128)S(1)} %get-tuple-element.11.own_ref), custom_call_target="tpu_custom_call" | custom-call | tf_op jit(solution)/shard_map/pallas_call | solution.py:498
  85.5 0.8 copy.14
  86.3 0.8 copy.13
  (1 shorter events, 0.0 us)
Async XLA Ops:
  0.6 34.0 %copy-start.2 = (bf16[128,24,128]{2,1,0:T(8,128)(2,1)S(1)}, bf16[128,24,128]{2,1,0:T(8,128)(2,1)}, u32[]{:S(2)}) copy-start(bf16[128,24,128]{2,1,0:T(8,128)(2,1)} %param.10) | copy-start | bytes 2359300
  0.6 34.0 %copy-start.1 = (bf16[128,24,128]{2,1,0:T(8,128)(2,1)S(1)}, bf16[128,24,128]{2,1,0:T(8,128)(2,1)}, u32[]{:S(2)}) copy-start(bf16[128,24,128]{2,1,0:T(8,128)(2,1)} %param.7) | copy-start | bytes 2359300
  55.8 2.2 %copy-start = (bf16[16,2,4,128,128]{4,3,2,1,0:T(8,128)(2,1)S(1)}, bf16[16,2,4,128,128]{4,3,2,1,0:T(8,128)(2,1)}, u32[]{:S(2)}) copy-start(bf16[16,2,4,128,128]{4,3,2,1,0:T(8,128)(2,1)} %get-tuple-element.10.terms_ref) | copy-start | bytes 12582916

commit v2 on v0

--- a/solution.py
+++ b/solution.py
@@ -1,6 +1,8 @@
 import jax
 import jax.numpy as jnp
 from jax import lax
+from jax.experimental import pallas as pl
+from jax.experimental.pallas import tpu as pltpu
 from jax.sharding import PartitionSpec as P
 
 
@@ -93,7 +95,7 @@
     return fetched[:, which].reshape(listed * rows, kv_count, width).transpose(1, 0, 2)
 
 
-def local(queries, key_heads, value_heads, grad_out, offsets, random_masks, global_blocks):
+def local_any(queries, key_heads, value_heads, grad_out, offsets, random_masks, global_blocks):
     rows, heads, width = queries.shape
     kv_count = key_heads.shape[1]
     grouped = heads // kv_count
@@ -139,9 +141,452 @@
     return (attended, grad_queries, grad_keys, grad_values)
 
 
+MESH = pl.DeviceIdType.MESH
+FLOAT = jnp.float32
+HALF = jnp.bfloat16
+FAR, SIDE, CORES = 4, 2, 2
+
+
+def place():
+    me = lax.axis_index("seq")
+    return me, me // 4, (me // 2) % 2, me % 2
+
+
+def neighbours(me, z, x, c):
+    sibling = me + 1 - 2 * c
+    across = me + 2 - 4 * x
+    return sibling, across, me + 4, me - 4
+
+
+def greet(me, z, x, c):
+    sibling, across, up, down = neighbours(me, z, x, c)
+    barrier = pltpu.get_barrier_semaphore()
+    for other in (sibling, across):
+        pl.semaphore_signal(barrier, inc=1, device_id={"seq": other}, device_id_type=MESH)
+
+    @pl.when(z < FAR - 1)
+    def _():
+        pl.semaphore_signal(barrier, inc=1, device_id={"seq": up}, device_id_type=MESH)
+
+    @pl.when(z > 0)
+    def _():
+        pl.semaphore_signal(barrier, inc=1, device_id={"seq": down}, device_id_type=MESH)
+
+    pl.semaphore_wait(barrier, 3 + (z + 1) // 2 % 2)
+
+
+def nt(a, b):
+    return lax.dot_general(a, b, (((1,), (1,)), ((), ())), preferred_element_type=FLOAT)
+
+
+def nn(a, b):
+    return lax.dot_general(a, b, (((1,), (0,)), ((), ())), preferred_element_type=FLOAT)
+
+
+def pick(codes, z):
+    packed = sum(code * 4**i for i, code in enumerate(codes))
+    return packed // ((1 + 3 * (z % 2)) * (1 + 15 * (z // 2))) % 4
+
+
+ORDER = ((3, 3, 0, 0), (2, 0, 3, 1), (1, 2, 1, 2), (0, 1, 2, 3))
+
+
+def layer_kernel(
+    chosen_ref, named_ref, q_ref, g_ref, kv_ref,
+    att_ref, dq_ref, out_ref,
+    qf, gf, af, df, sums, merged, all_first, all_second, own, keep, give,
+    from_core, from_side, from_up, from_down, to_side, to_row, acc,
+    own_sem, gather_side, gather_core, gather_up, gather_down, gather_recv,
+    core_send, side_send, row_send, core_recv, side_recv, up_recv, down_recv,
+):
+    me, z, x, c = place()
+    sibling, across, up, down = neighbours(me, z, x, c)
+    blocks = (all_first, all_second)
+    listed = chosen_ref.shape[0]
+    _, _, per_half, rows, width = kv_ref.shape
+    heads = q_ref.shape[0] // rows
+    grouped = heads // (2 * per_half)
+    pairs = grouped // 2
+    scale = width ** (-0.5)
+
+    def remote(src, dst, send, recv, target):
+        return pltpu.make_async_remote_copy(
+            src_ref=src, dst_ref=dst, send_sem=send, recv_sem=recv,
+            device_id={"seq": target}, device_id_type=MESH,
+        )
+
+    def copy(slot, half, sem, target, mine=False):
+        return remote(
+            kv_ref.at[half] if mine else blocks[half].at[slot], blocks[half].at[slot],
+            sem, gather_recv.at[slot, half], target,
+        )
+
+    def column(row):
+        return row * 4 + x * 2 + c
+
+    def opposite(row):
+        return row * 4 + (1 - x) * 2 + c
+
+    def arrived(slot, half):
+        copy(slot, half, gather_side.at[0, half], across).wait_recv()
+
+    def pass_on(row, half, upward, downward, mine=False):
+        slot = column(row)
+        copy(slot, half, gather_side.at[row, half], across, mine).start()
+        if upward:
+
+            @pl.when(z < FAR - 1)
+            def _():
+                copy(slot, half, gather_up.at[row, half], up, mine).start()
+
+        if downward:
+
+            @pl.when(z > 0)
+            def _():
+                copy(slot, half, gather_down.at[row, half], down, mine).start()
+
+        copy(slot, half, gather_core.at[0, row, half], sibling, mine).start()
+
+    def own_copy(half):
+        return pltpu.make_async_copy(kv_ref.at[half], blocks[half].at[me], own_sem.at[half])
+
+    def gather_start(half):
+        pass_on(z, half, True, True, mine=True)
+        own_copy(half).start()
+
+    def share(row, half):
+        arrived(opposite(row), half)
+        copy(opposite(row), half, gather_core.at[1, row, half], sibling).start()
+
+    def gather_shares(step, half):
+        if step == 0:
+            share(z, half)
+            return
+
+        @pl.when(z - step >= 0)
+        def _():
+            share(z - step, half)
+
+        @pl.when(z + step < FAR)
+        def _():
+            share(z + step, half)
+
+    def gather_step(step, half):
+        @pl.when(z - step >= 0)
+        def _():
+            arrived(column(z - step), half)
+            pass_on(z - step, half, True, False)
+
+        @pl.when(z + step < FAR)
+        def _():
+            arrived(column(z + step), half)
+            pass_on(z + step, half, False, True)
+
+    def gather_end(half):
+        for row in range(FAR):
+            for col in range(SIDE):
+                arrived(row * 4 + col * 2 + 1 - c, half)
+        own_copy(half).wait()
+
+    def gather_sent(half):
+        for row in range(FAR):
+            copy(column(row), half, gather_side.at[row, half], across).wait_send()
+            for which in range(2):
+                copy(column(row), half, gather_core.at[which, row, half], sibling).wait_send()
+
+            @pl.when((z < FAR - 1) & (z >= row))
+            def _(row=row):
+                copy(column(row), half, gather_up.at[row, half], up).wait_send()
+
+            @pl.when((z > 0) & (z <= row))
+            def _(row=row):
+                copy(column(row), half, gather_down.at[row, half], down).wait_send()
+
+    def attend(half, between):
+        fetched = blocks[half]
+
+        def one(head, _):
+            keys = jnp.concatenate([fetched[chosen_ref[i], 0, head] for i in range(listed)], axis=0)
+            values = jnp.concatenate(
+                [fetched[chosen_ref[i], 1, head] for i in range(listed)], axis=0
+            )
+            keys_t, values_t = keys.T, values.T
+            for pair in range(pairs):
+                first = (half * per_half + head) * grouped + 2 * pair
+                spans = [pl.ds(first + i, rows, stride=heads) for i in range(2)]
+                query = jnp.concatenate([qf[s, :] for s in spans], axis=0).astype(HALF)
+                grad = jnp.concatenate([gf[s, :] for s in spans], axis=0).astype(HALF)
+                scores = nt(keys, query)
+                top = jnp.max(scores, axis=0, keepdims=True)
+                weights = jnp.exp((scores - top) * scale)
+                weights = weights * (1.0 / jnp.sum(weights, axis=0, keepdims=True))
+                probs = weights.astype(HALF)
+                out = nn(values_t, probs).T
+                grad_probs = nt(values, grad)
+                deltas = jnp.sum(weights * grad_probs, axis=0, keepdims=True)
+                grad_scores = (weights * (grad_probs - deltas)).astype(HALF)
+                grad_query = (nn(keys_t, grad_scores) * scale).T
+                for i, s in enumerate(spans):
+                    af[s, :] = out[i * rows : (i + 1) * rows]
+                    df[s, :] = grad_query[i * rows : (i + 1) * rows]
+                key_terms = nn(grad_scores, query).reshape(listed, rows, width)
+                value_terms = nn(probs, grad).reshape(listed, rows, width)
+                if pair == 0:
+                    sums[:, 0] = key_terms
+                    sums[:, 1] = value_terms
+                else:
+                    sums[:, 0] += key_terms
+                    sums[:, 1] += value_terms
+                between(head, pair)
+            for which, factor in ((0, scale), (1, 1.0)):
+                own[half, which, head] = sums[0, which] * factor
+                for i in range(1, listed):
+                    total = sums[i, which]
+                    for j in range(1, listed):
+                        if j != i:
+                            same = chosen_ref[j] == chosen_ref[i]
+                            total = total + jnp.where(same, sums[j, which], 0.0)
+                    merged[i, which] = total * factor
+                merged[0, which] = jnp.zeros((rows, width), FLOAT)
+            for row in range(FAR):
+                for col in range(SIDE):
+                    slot = row * 4 + col * 2
+                    keep[half, row, col, :, head] = merged[named_ref[slot + c]]
+                    give[half, row, col, :, head] = merged[named_ref[slot + 1 - c]].astype(HALF)
+            return 0
+
+        lax.fori_loop(0, per_half, one, 0)
+
+    def core_copy(row, col, half):
+        return remote(
+            give.at[half, row, col], from_core.at[half, row, col],
+            core_send.at[half, row, col], core_recv.at[half, row, col], sibling,
+        )
+
+    def side_copy(row, half):
+        return remote(
+            to_side.at[half, row], from_side.at[half, row],
+            side_send.at[half, row], side_recv.at[half, row], across,
+        )
+
+    def up_copy(row, half):
+        return remote(
+            to_row.at[half, row], from_down.at[half, row],
+            row_send.at[half, row], down_recv.at[half, row], up,
+        )
+
+    def down_copy(row, half):
+        return remote(
+            to_row.at[half, row], from_up.at[half, row],
+            row_send.at[half, row], up_recv.at[half, row], down,
+        )
+
+    order = [pick(codes, z) for codes in ORDER]
+
+    def core_start(half):
+        for row in order:
+            core_copy(row, 1 - x, half).start()
+        for row in order:
+            core_copy(row, x, half).start()
+
+    def side_step(step, half):
+        row = order[step]
+        core_copy(row, 1 - x, half).wait_recv()
+        to_side[half, row] = (
+            keep[half, row, 1 - x] + from_core[half, row, 1 - x].astype(FLOAT)
+        ).astype(HALF)
+        side_copy(row, half).start()
+
+    def row_step(step, half):
+        row = order[step]
+        core_copy(row, x, half).wait_recv()
+        side_copy(row, half).wait_recv()
+        acc[...] = (
+            keep[half, row, x]
+            + from_core[half, row, x].astype(FLOAT)
+            + from_side[half, row].astype(FLOAT)
+        )
+
+        @pl.when((row >= z) & (z > 0))
+        def _():
+            up_copy(row, half).wait_recv()
+            acc[...] += from_down[half, row].astype(FLOAT)
+
+        @pl.when((row <= z) & (z < FAR - 1))
+        def _():
+            down_copy(row, half).wait_recv()
+            acc[...] += from_up[half, row].astype(FLOAT)
+
+        if step < FAR - 1:
+            to_row[half, row] = acc[...].astype(HALF)
+
+            @pl.when(row > z)
+            def _():
+                up_copy(row, half).start()
+
+            @pl.when(row < z)
+            def _():
+                down_copy(row, half).start()
+        else:
+            out_ref[half] = (acc[...] + own[half]).astype(HALF)
+
+    def sum_sent(half):
+        for step, row in enumerate(order):
+            side_copy(row, half).wait_send()
+            for col in range(SIDE):
+                core_copy(row, col, half).wait_send()
+            if step < FAR - 1:
+                up_copy(row, half).wait_send()
+
+    def schedule(actions):
+        def between(head, pair):
+            for (at_head, at_pair), action in actions.items():
+                if at_pair == pair:
+                    pl.when(head == at_head)(action)
+
+        return between
+
+    def during_first_a():
+        gather_step(3, 1)
+        gather_shares(0, 1)
+
+    def during_first_b():
+        gather_shares(1, 1)
+
+    def during_first_c():
+        gather_shares(2, 1)
+
+    def during_first_d():
+        gather_shares(3, 1)
+
+    def during_second_a():
+        side_step(0, 0)
+        side_step(1, 0)
+
+    def during_second_b():
+        side_step(2, 0)
+        side_step(3, 0)
+
+    greet(me, z, x, c)
+    gather_start(0)
+    gf[...] = g_ref[...].astype(FLOAT)
+    gather_step(1, 0)
+    gather_step(2, 0)
+    gather_start(1)
+    qf[...] = q_ref[...].astype(FLOAT)
+    gather_shares(0, 0)
+    gather_step(3, 0)
+    gather_shares(1, 0)
+    gather_step(1, 1)
+    gather_shares(2, 0)
+    gather_step(2, 1)
+    gather_shares(3, 0)
+    gather_end(0)
+    attend(
+        0,
+        schedule(
+            {
+                (0, 0): during_first_a,
+                (0, 1): during_first_b,
+                (1, 0): during_first_c,
+                (1, 1): during_first_d,
+            }
+        ),
+    )
+    core_start(0)
+    gather_end(1)
+    attend(
+        1,
+        schedule(
+            {
+                (0, 0): during_second_a,
+                (0, 1): during_second_b,
+                (1, 0): lambda: row_step(0, 0),
+                (1, 1): lambda: row_step(1, 0),
+                (1, 2): lambda: row_step(2, 0),
+            }
+        ),
+    )
+    core_start(1)
+    for step in range(FAR):
+        side_step(step, 1)
+    row_step(3, 0)
+    att_ref[...] = af[...].astype(HALF)
+    dq_ref[...] = df[...].astype(HALF)
+    for step in range(FAR):
+        row_step(step, 1)
+    for half in range(2):
+        gather_sent(half)
+        sum_sent(half)
+
+
+def layer(chosen, named, query_rows, grad_rows, kv):
+    total, width = query_rows.shape
+    _, _, per_half, rows, _ = kv.shape
+    listed = chosen.shape[0]
+    tile = kv.shape[1:]
+    dma = pltpu.SemaphoreType.DMA
+    whole = pl.BlockSpec(memory_space=pltpu.VMEM)
+    scalars = pl.BlockSpec(memory_space=pltpu.SMEM)
+    slots = pltpu.VMEM((2, FAR, *tile), HALF)
+    long = pltpu.VMEM((total, width), FLOAT)
+    fetched = pltpu.VMEM((FAR * SIDE * CORES, *tile), HALF)
+    by_slot = (2, FAR, SIDE)
+    return pl.pallas_call(
+        layer_kernel,
+        out_shape=(
+            jax.ShapeDtypeStruct((total, width), HALF),
+            jax.ShapeDtypeStruct((total, width), HALF),
+            jax.ShapeDtypeStruct(kv.shape, HALF),
+        ),
+        in_specs=[scalars, scalars, whole, whole, whole],
+        out_specs=(whole,) * 3,
+        scratch_shapes=[
+            long, long, long, long,
+            pltpu.VMEM((listed, 2, rows, width), FLOAT),
+            pltpu.VMEM((listed, 2, rows, width), FLOAT),
+            fetched, fetched,
+            pltpu.VMEM(kv.shape, FLOAT),
+            pltpu.VMEM((*by_slot, *tile), FLOAT),
+            pltpu.VMEM((*by_slot, *tile), HALF),
+            pltpu.VMEM((*by_slot, *tile), HALF),
+            slots, slots, slots, slots, slots,
+            pltpu.VMEM(tile, FLOAT),
+            dma((2,)), dma((FAR, 2)), dma((2, FAR, 2)), dma((FAR, 2)), dma((FAR, 2)),
+            dma((FAR * SIDE * CORES, 2)),
+            dma(by_slot), dma((2, FAR)), dma((2, FAR)),
+            dma(by_slot), dma((2, FAR)), dma((2, FAR)), dma((2, FAR)),
+        ],
+        compiler_params=pltpu.CompilerParams(
+            collective_id=0, has_side_effects=True, vmem_limit_bytes=56 * 2**20
+        ),
+    )(chosen, named, query_rows, grad_rows, kv)
+
+
+def local(queries, key_heads, value_heads, grad_out, offsets, random_masks, global_blocks):
+    rows, heads, width = queries.shape
+    kv_count = key_heads.shape[1]
+    me = lax.axis_index("seq").astype(jnp.int32)
+    chosen = jnp.concatenate([me[None], me ^ offsets, me ^ random_masks, global_blocks])
+    slots = jnp.arange(FAR * SIDE * CORES, dtype=jnp.int32)
+    named = jnp.zeros_like(slots)
+    for i in range(1, chosen.shape[0]):
+        named = jnp.where(slots == chosen[i], i, named)
+    kv = jnp.stack([key_heads, value_heads]).reshape(2, rows, 2, kv_count // 2, width)
+    attended, grad_queries, totals = layer(
+        chosen, named,
+        queries.reshape(rows * heads, width), grad_out.reshape(rows * heads, width),
+        kv.transpose(2, 0, 3, 1, 4),
+    )
+    totals = totals.transpose(1, 3, 0, 2, 4).reshape(2, rows, kv_count, width)
+    return (
+        attended.reshape(queries.shape), grad_queries.reshape(queries.shape), totals[0], totals[1]
+    )
+
+
 def solution(mesh):
     return jax.shard_map(
-        local,
+        local if mesh.shape["seq"] == FAR * SIDE * CORES else local_any,
         mesh=mesh,
         in_specs=(
             P(("groups", "seq"), None, None),

time: 328 us -> 84.5 us (0.26)
  waiting for transfers between devices: 165 us -> 0 us
  local copies, waits for them, and re-layouts: 102 us -> 7.11 us
  Pallas kernels: 0 us -> 71.9 us
  between operations: 20.7 us -> 1.98 us
  matrix products: 18.1 us -> 0 us
  starting transfers between devices: 13.3 us -> 0 us
  other arithmetic: 9.57 us -> 3.24 us
    ppermute x10 -> x0, waiting for transfers between devices: 96.2 us -> none  [from_partner(): lax.ppermute(x, axis, [(i, i ^ 1 << distance) for i in range(lax.axis_siz...]
    dynamic_update_slice x8 -> x0, local copies, waits for them, and re-layouts: 75.9 us -> none  [local(): lax.map(backward_head, (query_part, head_major(fetched, 0), head_major(fe...]
    pallas_call x0 -> x1, Pallas kernels: none -> 71.9 us  [layer(): pl.pallas_call(layer_kernel, out_shape=(jax.ShapeDtypeStruct((total, widt...]
    psum x2 -> x0, waiting for transfers between devices: 69.1 us -> none  [the longest x1 41.2 us: local(): summed = lax.psum(terms[1 + routed_count:], 'seq')]
    dot_general x28 -> x0, matrix products: 18.1 us -> none  [the longest x4 4.75 us: forward_head(): jnp.einsum('pqk,kd->qpd', probs, value_part, preferred_element_type=jnp.f...]
    ppermute x10 -> x0, starting transfers between devices: 13.2 us -> none  [from_partner(): lax.ppermute(x, axis, [(i, i ^ 1 << distance) for i in range(lax.axis_siz...]
    cond x8 -> x0, local copies, waits for them, and re-layouts: 5.57 us -> none
    dynamic_slice x8 -> x0, local copies, waits for them, and re-layouts: 4.44 us -> none  [local(): lax.map(forward_head, (query_part, head_major(fetched, 0), head_major(fet...]
  transfers between devices with their start and end apart: 12 -> 0, of which waited for: 12 -> 0; matrix products, arithmetic and copies ran while one was open for 5% -> 0% of each run, Pallas kernels for 0% -> 0%
where the time goes in v2:
time: 84.5 us; the launch traced here: 84.2 us
  Pallas kernels  71.9 us (85%)
  local copies, waits for them, and re-layouts  7.11 us (8%)
  other arithmetic  3.24 us (4%)
  between operations  1.98 us (2%)
    pallas_call x1, Pallas kernels, layer(): pl.pallas_call(layer_kernel, out_shape=(jax.ShapeDtypeStruct((total, widt...  71.9 us
    unnamed x14, local copies, waits for them, and re-layouts  5.45 us
    select_n x1, other arithmetic, local(): named = jnp.where(slots == chosen[i], i, named)  1.92 us

profile of v2, /device:TPU:0, one launch (start us, length us, event | category | flops | bytes accessed | tf_op | source)
XLA Modules:
  0.0 84.2 jit_solution(16016166163438669676)
XLA Ops:
  1.9 0.0 copy-start.3
  1.9 0.6 copy-done.3
  2.6 0.6 pad_add_fusion.chosen_ref
  3.2 0.6 fusion.1
  3.8 1.9 %compare_select_fusion.3.named_ref = s32[16]{0:T(128)} fusion(s32[]{:T(128)} %bitcast.4, s32[]{:T(128)} %bitcast.3, s32[]{:T(128)} %bitcast.2, s32[]{:T(128)} %bitcast.16), kind=kLoop, calls=%fused_computation.4 | loop fusion | flops 128 | bytes 80 | tf_op jit(solution)/shard_map/jit(_where)/select_n | solution.py:574
  5.7 0.0 copy-start.2
  5.7 1.0 %copy.11 = bf16[128,4,128]{2,0,1:T(8,128)(2,1)S(1)} copy(bf16[128,4,128]{2,1,0:T(4,128)(2,1)} %param.8) | data formatting | bytes 262144 | tf_op args[1]
  6.7 0.0 copy-done.2
  6.7 0.7 maximum_bitcast_fusion.kv_ref
  7.4 71.9 %shard_map.102 = (bf16[3072,128]{1,0:T(8,128)(2,1)}, bf16[3072,128]{1,0:T(8,128)(2,1)}, bf16[2,2,2,128,128]{4,3,2,1,0:T(8,128)(2,1)}) custom-call(s32[5]{0:T(128)} %pad_add_fusion.chosen_ref, s32[16]{0:T(128)} %compare_select_fusion.3.named_ref, bf16[3072,128]{1,0:T(8,128)(2,1)} %bitcast.17, bf16[3072,128]{1,0:T(8,128)(2,1)} %bitcast.18, ...), custom_call_target="tpu_custom_call" | custom-call | tf_op jit(solution)/shard_map/pallas_call | solution.py:535
  79.3 0.0 copy-start.1
  79.3 1.1 %fusion = (bf16[1,128,2,2,128]{4,1,3,0,2:T(8,128)(2,1)S(1)}, bf16[1,128,2,2,128]{4,1,3,0,2:T(8,128)(2,1)S(1)}) fusion(bf16[2,128,2,2,128]{4,1,3,0,2:T(8,128)(2,1)} %bitcast.25), kind=kLoop, calls=%fused_computation.7 | loop fusion | bytes 524288 | tf_op jit(solution)/shard_map/slice | solution.py:583
  80.4 0.8 copy.14
  81.1 0.8 copy.13
  81.9 0.0 copy-done.1
  81.9 0.0 copy-start
  81.9 0.9 %copy.19 = bf16[128,24,128]{2,1,0:T(8,128)(2,1)} copy(bf16[128,24,128]{2,1,0:T(8,128)(2,1)S(1)} %bitcast.20) | data formatting | bytes 1572864
  82.8 0.5 copy-done
  83.3 0.9 %copy.20 = bf16[128,24,128]{2,1,0:T(8,128)(2,1)} copy(bf16[128,24,128]{2,1,0:T(8,128)(2,1)S(1)} %bitcast.19) | data formatting | bytes 1572864
  (2 shorter events, 0.0 us)
Async XLA Ops:
  1.9 0.7 copy-start.3
  5.7 1.0 %copy-start.2 = (bf16[128,4,128]{2,1,0:T(4,128)(2,1)S(1)}, bf16[128,4,128]{2,1,0:T(4,128)(2,1)}, u32[]{:S(2)}) copy-start(bf16[128,4,128]{2,1,0:T(4,128)(2,1)} %param.9) | copy-start | bytes 393220
  79.3 2.6 %copy-start.1 = (bf16[3072,128]{1,0:T(8,128)(2,1)S(1)}, bf16[3072,128]{1,0:T(8,128)(2,1)}, u32[]{:S(2)}) copy-start(bf16[3072,128]{1,0:T(8,128)(2,1)} %get-tuple-element.7) | copy-start | bytes 2359300
  81.9 1.4 %copy-start = (bf16[3072,128]{1,0:T(8,128)(2,1)S(1)}, bf16[3072,128]{1,0:T(8,128)(2,1)}, u32[]{:S(2)}) copy-start(bf16[3072,128]{1,0:T(8,128)(2,1)} %get-tuple-element.8) | copy-start | bytes 2359300

commit v3 on v0

--- a/solution.py
+++ b/solution.py
@@ -1,6 +1,8 @@
 import jax
 import jax.numpy as jnp
 from jax import lax
+from jax.experimental import pallas as pl
+from jax.experimental.pallas import tpu as pltpu
 from jax.sharding import PartitionSpec as P
 
 
@@ -93,7 +95,7 @@
     return fetched[:, which].reshape(listed * rows, kv_count, width).transpose(1, 0, 2)
 
 
-def local(queries, key_heads, value_heads, grad_out, offsets, random_masks, global_blocks):
+def local_any(queries, key_heads, value_heads, grad_out, offsets, random_masks, global_blocks):
     rows, heads, width = queries.shape
     kv_count = key_heads.shape[1]
     grouped = heads // kv_count
@@ -139,9 +141,436 @@
     return (attended, grad_queries, grad_keys, grad_values)
 
 
+MESH = pl.DeviceIdType.MESH
+FLOAT = jnp.float32
+HALF = jnp.bfloat16
+FAR, SIDE, CORES = 4, 2, 2
+
+
+def place():
+    me = lax.axis_index("seq")
+    return me, me // 4, (me // 2) % 2, me % 2
+
+
+def neighbours(me, z, x, c):
+    sibling = me + 1 - 2 * c
+    across = me + 2 - 4 * x
+    return sibling, across, me + 4, me - 4
+
+
+def greet(me, z, x, c):
+    sibling, across, up, down = neighbours(me, z, x, c)
+    barrier = pltpu.get_barrier_semaphore()
+    for other in (sibling, across):
+        pl.semaphore_signal(barrier, inc=1, device_id={"seq": other}, device_id_type=MESH)
+
+    @pl.when(z < FAR - 1)
+    def _():
+        pl.semaphore_signal(barrier, inc=1, device_id={"seq": up}, device_id_type=MESH)
+
+    @pl.when(z > 0)
+    def _():
+        pl.semaphore_signal(barrier, inc=1, device_id={"seq": down}, device_id_type=MESH)
+
+    pl.semaphore_wait(barrier, 3 + (z + 1) // 2 % 2)
+
+
+def nt(a, b):
+    return lax.dot_general(a, b, (((1,), (1,)), ((), ())), preferred_element_type=FLOAT)
+
+
+def nn(a, b):
+    return lax.dot_general(a, b, (((1,), (0,)), ((), ())), preferred_element_type=FLOAT)
+
+
+def pick(codes, z):
+    packed = sum(code * 4**i for i, code in enumerate(codes))
+    return packed // ((1 + 3 * (z % 2)) * (1 + 15 * (z // 2))) % 4
+
+
+ORDER = ((3, 3, 0, 0), (2, 0, 3, 1), (1, 2, 1, 2), (0, 1, 2, 3))
+
+
+def layer_kernel(
+    offsets_ref, masks_ref, globals_ref, q_ref, g_ref, kv_ref,
+    att_ref, dq_ref, dk_ref, dv_ref,
+    qf, gf, af, df, sums, merged, all_0, all_1, all_2, all_3, own, keep, give,
+    from_core, from_side, from_up, from_down, to_side, to_row, acc,
+    own_sem, gather_side, gather_core, gather_up, gather_down, gather_recv,
+    core_send, side_send, row_send, core_recv, side_recv, up_recv, down_recv,
+):
+    me, z, x, c = place()
+    sibling, across, up, down = neighbours(me, z, x, c)
+    blocks = (all_0, all_1, all_2, all_3)
+    chosen = [me]
+    chosen += [me ^ offsets_ref[i] for i in range(offsets_ref.shape[0])]
+    chosen += [me ^ masks_ref[i] for i in range(masks_ref.shape[0])]
+    chosen += [globals_ref[i] for i in range(globals_ref.shape[0])]
+    listed = len(chosen)
+    parts, _, rows, width = kv_ref.shape
+    heads = q_ref.shape[0] // rows
+    grouped = heads // parts
+    pairs = grouped // 2
+    scale = width ** (-0.5)
+
+    def remote(src, dst, send, recv, target):
+        return pltpu.make_async_remote_copy(
+            src_ref=src, dst_ref=dst, send_sem=send, recv_sem=recv,
+            device_id={"seq": target}, device_id_type=MESH,
+        )
+
+    def copy(slot, part, sem, target, mine=False):
+        return remote(
+            kv_ref.at[part] if mine else blocks[part].at[slot], blocks[part].at[slot],
+            sem, gather_recv.at[slot, part], target,
+        )
+
+    def column(row):
+        return row * 4 + x * 2 + c
+
+    def opposite(row):
+        return row * 4 + (1 - x) * 2 + c
+
+    def arrived(slot, part):
+        copy(slot, part, gather_side.at[0, part], across).wait_recv()
+
+    def pass_on(row, part, upward, downward, mine=False):
+        slot = column(row)
+        copy(slot, part, gather_side.at[row, part], across, mine).start()
+        if upward:
+
+            @pl.when(z < FAR - 1)
+            def _():
+                copy(slot, part, gather_up.at[row, part], up, mine).start()
+
+        if downward:
+
+            @pl.when(z > 0)
+            def _():
+                copy(slot, part, gather_down.at[row, part], down, mine).start()
+
+        copy(slot, part, gather_core.at[0, row, part], sibling, mine).start()
+
+    def own_copy(part):
+        return pltpu.make_async_copy(kv_ref.at[part], blocks[part].at[me], own_sem.at[part])
+
+    def gather_start(part):
+        pass_on(z, part, True, True, mine=True)
+        own_copy(part).start()
+
+    def share(row, part):
+        arrived(opposite(row), part)
+        copy(opposite(row), part, gather_core.at[1, row, part], sibling).start()
+
+    def gather_shares(step, part):
+        if step == 0:
+            share(z, part)
+            return
+
+        @pl.when(z - step >= 0)
+        def _():
+            share(z - step, part)
+
+        @pl.when(z + step < FAR)
+        def _():
+            share(z + step, part)
+
+    def gather_step(step, part):
+        @pl.when(z - step >= 0)
+        def _():
+            arrived(column(z - step), part)
+            pass_on(z - step, part, True, False)
+
+        @pl.when(z + step < FAR)
+        def _():
+            arrived(column(z + step), part)
+            pass_on(z + step, part, False, True)
+
+    def gather_end(part):
+        for row in range(FAR):
+            for col in range(SIDE):
+                arrived(row * 4 + col * 2 + 1 - c, part)
+        own_copy(part).wait()
+
+    def gather_sent(part):
+        for row in range(FAR):
+            copy(column(row), part, gather_side.at[row, part], across).wait_send()
+            for which in range(2):
+                copy(column(row), part, gather_core.at[which, row, part], sibling).wait_send()
+
+            @pl.when((z < FAR - 1) & (z >= row))
+            def _(row=row):
+                copy(column(row), part, gather_up.at[row, part], up).wait_send()
+
+            @pl.when((z > 0) & (z <= row))
+            def _(row=row):
+                copy(column(row), part, gather_down.at[row, part], down).wait_send()
+
+    def named(slot):
+        entry = 0
+        for i in range(1, listed):
+            entry = jnp.where(chosen[i] == slot, i, entry)
+        return entry
+
+    def attend(part, *between):
+        fetched = blocks[part]
+        keys = jnp.concatenate([fetched[block, 0] for block in chosen], axis=0)
+        values = jnp.concatenate([fetched[block, 1] for block in chosen], axis=0)
+        keys_t, values_t = keys.T, values.T
+        for pair in range(pairs):
+            first = part * grouped + 2 * pair
+            spans = [pl.ds(first + i, rows, stride=heads) for i in range(2)]
+            query = jnp.concatenate([qf[s, :] for s in spans], axis=0).astype(HALF)
+            grad = jnp.concatenate([gf[s, :] for s in spans], axis=0).astype(HALF)
+            scores = nt(keys, query)
+            top = jnp.max(scores, axis=0, keepdims=True)
+            weights = jnp.exp((scores - top) * scale)
+            weights = weights * (1.0 / jnp.sum(weights, axis=0, keepdims=True))
+            probs = weights.astype(HALF)
+            out = nn(values_t, probs).T
+            grad_probs = nt(values, grad)
+            deltas = jnp.sum(weights * grad_probs, axis=0, keepdims=True)
+            grad_scores = (weights * (grad_probs - deltas)).astype(HALF)
+            grad_query = (nn(keys_t, grad_scores) * scale).T
+            for i, s in enumerate(spans):
+                af[s, :] = out[i * rows : (i + 1) * rows]
+                df[s, :] = grad_query[i * rows : (i + 1) * rows]
+            key_terms = nn(grad_scores, query).reshape(listed, rows, width)
+            value_terms = nn(probs, grad).reshape(listed, rows, width)
+            if pair == 0:
+                sums[:, 0] = key_terms
+                sums[:, 1] = value_terms
+            else:
+                sums[:, 0] += key_terms
+                sums[:, 1] += value_terms
+            for action, *at in between[pair] if pair < len(between) else ():
+                action(*at)
+        for which, factor in ((0, scale), (1, 1.0)):
+            own[part, which] = sums[0, which] * factor
+            for i in range(1, listed):
+                total = sums[i, which]
+                for j in range(1, listed):
+                    if j != i:
+                        same = chosen[j] == chosen[i]
+                        total = total + jnp.where(same, sums[j, which], 0.0)
+                merged[i, which] = total * factor
+            merged[0, which] = jnp.zeros((rows, width), FLOAT)
+        for row in range(FAR):
+            for col in range(SIDE):
+                slot = row * 4 + col * 2
+                keep[part, row, col] = merged[named(slot + c)]
+                give[part, row, col] = merged[named(slot + 1 - c)].astype(HALF)
+
+    def core_copy(row, col, part):
+        return remote(
+            give.at[part, row, col], from_core.at[part, row, col],
+            core_send.at[part, row, col], core_recv.at[part, row, col], sibling,
+        )
+
+    def side_copy(row, part):
+        return remote(
+            to_side.at[part, row], from_side.at[part, row],
+            side_send.at[part, row], side_recv.at[part, row], across,
+        )
+
+    def up_copy(row, part):
+        return remote(
+            to_row.at[part, row], from_down.at[part, row],
+            row_send.at[part, row], down_recv.at[part, row], up,
+        )
+
+    def down_copy(row, part):
+        return remote(
+            to_row.at[part, row], from_up.at[part, row],
+            row_send.at[part, row], up_recv.at[part, row], down,
+        )
+
+    order = [pick(codes, z) for codes in ORDER]
+
+    def core_start(part):
+        for row in order:
+            core_copy(row, 1 - x, part).start()
+        for row in order:
+            core_copy(row, x, part).start()
+
+    def side_step(step, part):
+        row = order[step]
+        core_copy(row, 1 - x, part).wait_recv()
+        to_side[part, row] = (
+            keep[part, row, 1 - x] + from_core[part, row, 1 - x].astype(FLOAT)
+        ).astype(HALF)
+        side_copy(row, part).start()
+
+    def row_step(step, part):
+        row = order[step]
+        core_copy(row, x, part).wait_recv()
+        side_copy(row, part).wait_recv()
+        acc[...] = (
+            keep[part, row, x]
+            + from_core[part, row, x].astype(FLOAT)
+            + from_side[part, row].astype(FLOAT)
+        )
+
+        @pl.when((row >= z) & (z > 0))
+        def _():
+            up_copy(row, part).wait_recv()
+            acc[...] += from_down[part, row].astype(FLOAT)
+
+        @pl.when((row <= z) & (z < FAR - 1))
+        def _():
+            down_copy(row, part).wait_recv()
+            acc[...] += from_up[part, row].astype(FLOAT)
+
+        if step < FAR - 1:
+            to_row[part, row] = acc[...].astype(HALF)
+
+            @pl.when(row > z)
+            def _():
+                up_copy(row, part).start()
+
+            @pl.when(row < z)
+            def _():
+                down_copy(row, part).start()
+        else:
+            dk_ref[part] = (acc[0] + own[part, 0]).astype(HALF)
+            dv_ref[part] = (acc[1] + own[part, 1]).astype(HALF)
+
+    def sum_sent(part):
+        for step, row in enumerate(order):
+            side_copy(row, part).wait_send()
+            for col in range(SIDE):
+                core_copy(row, col, part).wait_send()
+            if step < FAR - 1:
+                up_copy(row, part).wait_send()
+
+    def side_steps(part):
+        for step in range(FAR):
+            side_step(step, part)
+
+    start, hop, shares = gather_start, gather_step, gather_shares
+    greet(me, z, x, c)
+    start(0)
+    start(1)
+    gf[...] = g_ref[...].astype(FLOAT)
+    hop(1, 0)
+    shares(0, 0)
+    hop(2, 0)
+    shares(1, 0)
+    hop(3, 0)
+    start(2)
+    qf[...] = q_ref[...].astype(FLOAT)
+    shares(2, 0)
+    hop(1, 1)
+    shares(0, 1)
+    hop(2, 1)
+    shares(3, 0)
+    gather_end(0)
+    attend(
+        0,
+        [(hop, 3, 1), (start, 3), (shares, 1, 1)],
+        [(hop, 1, 2), (shares, 0, 2), (shares, 2, 1), (hop, 2, 2)],
+        [(shares, 3, 1), (hop, 3, 2), (hop, 1, 3), (shares, 1, 2)],
+    )
+    core_start(0)
+    gather_end(1)
+    attend(
+        1,
+        [(hop, 2, 3), (shares, 2, 2), (shares, 0, 3), (side_steps, 0)],
+        [(shares, 3, 2), (hop, 3, 3), (shares, 1, 3)],
+        [(shares, 2, 3), (row_step, 0, 0)],
+    )
+    core_start(1)
+    gather_end(2)
+    attend(
+        2,
+        [(shares, 3, 3), (side_steps, 1)],
+        [(row_step, 1, 0), (row_step, 2, 0)],
+        [(row_step, 3, 0), (row_step, 0, 1)],
+    )
+    core_start(2)
+    gather_end(3)
+    attend(
+        3,
+        [(side_steps, 2), (row_step, 1, 1)],
+        [(row_step, 2, 1), (row_step, 3, 1)],
+        [(row_step, 0, 2), (row_step, 1, 2)],
+    )
+    core_start(3)
+    row_step(2, 2)
+    side_steps(3)
+    row_step(3, 2)
+    att_ref[...] = af[...].astype(HALF)
+    dq_ref[...] = df[...].astype(HALF)
+    for step in range(FAR):
+        row_step(step, 3)
+    for part in range(parts):
+        gather_sent(part)
+        sum_sent(part)
+
+
+def layer(offsets, masks, global_blocks, query_rows, grad_rows, kv):
+    total, width = query_rows.shape
+    parts, _, rows, _ = kv.shape
+    listed = 1 + offsets.shape[0] + masks.shape[0] + global_blocks.shape[0]
+    tile = kv.shape[1:]
+    dma = pltpu.SemaphoreType.DMA
+    whole = pl.BlockSpec(memory_space=pltpu.VMEM)
+    scalars = pl.BlockSpec(memory_space=pltpu.SMEM)
+    slots = pltpu.VMEM((parts, FAR, *tile), HALF)
+    long = pltpu.VMEM((total, width), FLOAT)
+    fetched = pltpu.VMEM((FAR * SIDE * CORES, *tile), HALF)
+    by_slot = (parts, FAR, SIDE)
+    grad_shape = jax.ShapeDtypeStruct((parts, rows, width), HALF)
+    return pl.pallas_call(
+        layer_kernel,
+        out_shape=(
+            jax.ShapeDtypeStruct((total, width), HALF),
+            jax.ShapeDtypeStruct((total, width), HALF),
+            grad_shape,
+            grad_shape,
+        ),
+        in_specs=[scalars, scalars, scalars, whole, whole, whole],
+        out_specs=(whole,) * 4,
+        scratch_shapes=[
+            long, long, long, long,
+            pltpu.VMEM((listed, 2, rows, width), FLOAT),
+            pltpu.VMEM((listed, 2, rows, width), FLOAT),
+            fetched, fetched, fetched, fetched,
+            pltpu.VMEM(kv.shape, FLOAT),
+            pltpu.VMEM((*by_slot, *tile), FLOAT),
+            pltpu.VMEM((*by_slot, *tile), HALF),
+            pltpu.VMEM((*by_slot, *tile), HALF),
+            slots, slots, slots, slots, slots,
+            pltpu.VMEM(tile, FLOAT),
+            dma((parts,)), dma((FAR, parts)), dma((2, FAR, parts)), dma((FAR, parts)),
+            dma((FAR, parts)), dma((FAR * SIDE * CORES, parts)),
+            dma(by_slot), dma((parts, FAR)), dma((parts, FAR)),
+            dma(by_slot), dma((parts, FAR)), dma((parts, FAR)), dma((parts, FAR)),
+        ],
+        compiler_params=pltpu.CompilerParams(
+            collective_id=0, has_side_effects=True, vmem_limit_bytes=56 * 2**20
+        ),
+    )(offsets, masks, global_blocks, query_rows, grad_rows, kv)
+
+
+def local(queries, key_heads, value_heads, grad_out, offsets, random_masks, global_blocks):
+    rows, heads, width = queries.shape
+    kv = jnp.stack([key_heads, value_heads]).transpose(2, 0, 1, 3)
+    attended, grad_queries, grad_keys, grad_values = layer(
+        offsets, random_masks, global_blocks,
+        queries.reshape(rows * heads, width), grad_out.reshape(rows * heads, width), kv,
+    )
+    return (
+        attended.reshape(queries.shape),
+        grad_queries.reshape(queries.shape),
+        grad_keys.transpose(1, 0, 2),
+        grad_values.transpose(1, 0, 2),
+    )
+
+
 def solution(mesh):
     return jax.shard_map(
-        local,
+        local if mesh.shape["seq"] == FAR * SIDE * CORES else local_any,
         mesh=mesh,
         in_specs=(
             P(("groups", "seq"), None, None),

time: 328 us -> 93.4 us (0.28)
  waiting for transfers between devices: 165 us -> 0 us
  local copies, waits for them, and re-layouts: 102 us -> 6.51 us
  Pallas kernels: 0 us -> 84 us
  between operations: 20.7 us -> 1.95 us
  matrix products: 18.1 us -> 0 us
  starting transfers between devices: 13.3 us -> 0 us
  other arithmetic: 9.57 us -> 0.73 us
    ppermute x10 -> x0, waiting for transfers between devices: 96.2 us -> none  [from_partner(): lax.ppermute(x, axis, [(i, i ^ 1 << distance) for i in range(lax.axis_siz...]
    pallas_call x0 -> x1, Pallas kernels: none -> 84 us  [layer(): pl.pallas_call(layer_kernel, out_shape=(jax.ShapeDtypeStruct((total, widt...]
    dynamic_update_slice x8 -> x0, local copies, waits for them, and re-layouts: 75.9 us -> none  [local(): lax.map(backward_head, (query_part, head_major(fetched, 0), head_major(fe...]
    psum x2 -> x0, waiting for transfers between devices: 69.1 us -> none  [the longest x1 41.2 us: local(): summed = lax.psum(terms[1 + routed_count:], 'seq')]
    dot_general x28 -> x0, matrix products: 18.1 us -> none  [the longest x4 4.75 us: forward_head(): jnp.einsum('pqk,kd->qpd', probs, value_part, preferred_element_type=jnp.f...]
    ppermute x10 -> x0, starting transfers between devices: 13.2 us -> none  [from_partner(): lax.ppermute(x, axis, [(i, i ^ 1 << distance) for i in range(lax.axis_siz...]
    cond x8 -> x0, local copies, waits for them, and re-layouts: 5.57 us -> none
    dynamic_slice x8 -> x0, local copies, waits for them, and re-layouts: 4.44 us -> none  [local(): lax.map(forward_head, (query_part, head_major(fetched, 0), head_major(fet...]
  transfers between devices with their start and end apart: 12 -> 0, of which waited for: 12 -> 0; matrix products, arithmetic and copies ran while one was open for 5% -> 0% of each run, Pallas kernels for 0% -> 0%
where the time goes in v3:
time: 93.4 us; the launch traced here: 93.2 us
  Pallas kernels  84 us (90%)
  local copies, waits for them, and re-layouts  6.51 us (7%)
  between operations  1.95 us (2%)
    pallas_call x1, Pallas kernels, layer(): pl.pallas_call(layer_kernel, out_shape=(jax.ShapeDtypeStruct((total, widt...  84 us
    unnamed x8, local copies, waits for them, and re-layouts  5.51 us

profile of v3, /device:TPU:0, one launch (start us, length us, event | category | flops | bytes accessed | tf_op | source)
XLA Modules:
  0.0 93.2 jit_solution(15382853961786489132)
XLA Ops:
  1.9 1.0 %copy_bitcast_fusion = (bf16[1,128,4,128]{3,1,0,2:T(8,128)(2,1)S(1)}, bf16[1,128,4,128]{3,1,0,2:T(8,128)(2,1)S(1)}) fusion(bf16[128,4,128]{2,1,0:T(4,128)(2,1)} %param.9, bf16[128,4,128]{2,1,0:T(4,128)(2,1)} %param.8), kind=kLoop, calls=%fused_computation.1 | loop fusion | bytes 524288 | tf_op jit(solution)/shard_map/stack | solution.py:558
  2.9 0.7 maximum_bitcast_fusion.kv_ref
  3.7 84.0 %shard_map.102 = (bf16[3072,128]{1,0:T(8,128)(2,1)}, bf16[3072,128]{1,0:T(8,128)(2,1)}, bf16[4,128,128]{2,1,0:T(8,128)(2,1)}, bf16[4,128,128]{2,1,0:T(8,128)(2,1)}) custom-call(s32[2]{0:T(128)} %offsets_ref.1, s32[1]{0:T(128)S(6)} %copy.19.masks_ref, s32[1]{0:T(128)S(6)} %copy.20.globals_ref, bf16[3072,128]{1,0:T(8,128)(2,1)} %bitcast.14, ...), custom_call_target="tpu_custom_call" | custom-call | tf_op jit(solution)/shard_map/pallas_call | solution.py:524
  87.7 0.0 copy-start.1
  87.7 1.7 %copy.13 = bf16[128,4,128]{2,1,0:T(4,128)(2,1)} copy(bf16[128,4,128]{2,0,1:T(8,128)(2,1)} %bitcast.17) | data formatting | bytes 262144
  89.4 0.0 copy-done.1
  89.4 0.8 copy.14
  90.2 0.0 copy-start
  90.2 2.2 %copy.21 = bf16[128,24,128]{2,1,0:T(8,128)(2,1)} copy(bf16[128,24,128]{2,1,0:T(8,128)(2,1)} %bitcast.13) | data formatting | bytes 1572864
  92.3 0.0 copy-done
  92.3 0.9 copy.22
Async XLA Ops:
  87.7 1.7 %copy-start.1 = (bf16[4,128,128]{2,1,0:T(8,128)(2,1)S(1)}, bf16[4,128,128]{2,1,0:T(8,128)(2,1)}, u32[]{:S(2)}) copy-start(bf16[4,128,128]{2,1,0:T(8,128)(2,1)} %get-tuple-element.11) | copy-start | bytes 393220
  90.2 2.2 %copy-start = (bf16[3072,128]{1,0:T(8,128)(2,1)S(1)}, bf16[3072,128]{1,0:T(8,128)(2,1)}, u32[]{:S(2)}) copy-start(bf16[3072,128]{1,0:T(8,128)(2,1)} %get-tuple-element.9) | copy-start | bytes 2359300
